TPU v7x, 256 devices: a whole 4x4x8 slice. The times are simulated.
256 devices in a mesh: row: 2 (over core), col: 8 (over z), depth: 16 (over y, x).
Axes of the slice: x: 4, y: 4, z: 8, core: 2. Of those that a mesh axis runs over, the one named last changes fastest.
Arguments:
- gram_slab: float32 [32, 2, 256, 2, 8, 256], P(None, 'row', None, None, 'col'), may hold values from -1537 to 2561, as said below
Outputs:
- factored: float32 [32, 2, 256, 2, 8, 256], P('depth', 'row', None, None, 'col')
Inputs may be any that keep to these rules, and one draw needn't show every extreme that they name: `gram_slab`: the top 4096 rows of S form a symmetric block, and its leading 2 * 256 rows and columns are positive definite.
All inputs are finite; a program needn't handle non-finite values.
Results may differ from a plain program's by a relative error of at most 0.0001.
Values sent between devices are 32-bit elements; how exact they have to be, the bound alone decides.
No kernel may reach another device: no remote copies, remote signals or barrier semaphores. Data moves between devices by JAX's collectives and lax.ppermute only.
A program may use at most 192 MiB of HBM per device.

v0:
```python
import jax
import jax.numpy as jnp
from jax import lax
from jax.sharding import PartitionSpec as P

highest = lax.Precision.HIGHEST


def from_root(block, axis, owner):
    block = jnp.where(lax.axis_index(axis) == owner, block, jnp.zeros_like(block))
    return lax.psum(block, axis)


def project(inverse_rows, column):
    return jnp.einsum("kv,auv->kau", inverse_rows, column, precision=highest)


def outer_update(lower_rows, col_tiles):
    return -jnp.einsum("kau,kcv->aucv", lower_rows, col_tiles, precision=highest)


def rows_from(panel_rows, row_ids, panel_id):
    return panel_rows * (row_ids >= panel_id).astype(jnp.float32)[None, :, None]


def rows_after(panel_rows, row_ids, panel_id):
    return panel_rows * (row_ids > panel_id).astype(jnp.float32)[None, :, None]


def apply_update(updates, panel_id, panel_rows, row_ids, col_tiles, col_ids, col_start, col_stop):
    lower_rows = rows_after(panel_rows, row_ids, panel_id)
    live_cols = (col_ids > panel_id).astype(jnp.float32)
    change = outer_update(lower_rows, col_tiles) * live_cols[None, None, :, None]
    return updates.at[:, :, col_start:col_stop, :].add(change)


def shards(gram_slab):
    tile_rows = gram_slab.shape[0]
    tile_size = gram_slab.shape[2]
    tile_cols = gram_slab.shape[3]
    row_count = lax.axis_size("row")
    col_count = lax.axis_size("col")
    depth_count = lax.axis_size("depth")
    row_id = lax.axis_index("row")
    col_id = lax.axis_index("col")
    depth_id = lax.axis_index("depth")
    matrix = gram_slab.reshape(tile_rows, tile_size, tile_cols, tile_size)
    global_rows = jnp.arange(tile_rows, dtype=jnp.int32) * row_count + row_id
    global_cols = jnp.arange(tile_cols, dtype=jnp.int32) * col_count + col_id
    identity = jnp.eye(tile_size, dtype=jnp.float32)
    is_first = (global_cols == 0)[None, None, :, None]
    is_second = (global_cols == 1)[None, None, :, None]

    def pivot_inverse(panel_id, pivot_local):
        pivot_block = from_root(pivot_local, "row", panel_id % row_count)
        is_owner = col_id == panel_id % col_count
        pivot_block = jnp.where(is_owner, pivot_block, identity)
        factor = jnp.linalg.cholesky(pivot_block)
        return jax.scipy.linalg.solve_triangular(factor, identity, lower=True)

    depth_share = tile_size // depth_count
    first_depth = (depth_id == 0).astype(jnp.float32)

    def rank_panel(panel_id, updates):
        local_col = panel_id // col_count
        column = matrix[:, :, local_col, :]
        if panel_id > 0:
            column = column + lax.psum(updates[:, :, local_col, :], "depth")
        inverse = pivot_inverse(panel_id, column[panel_id // row_count])
        inverse_part = lax.dynamic_slice_in_dim(inverse, depth_id * depth_share, depth_share, 0)
        panel_rows = rows_from(project(inverse_part, column), global_rows, panel_id)
        panel_rows = from_root(panel_rows, "col", panel_id % col_count)
        groups = tile_rows // col_count
        own_pieces = lax.dynamic_slice_in_dim(
            panel_rows.reshape(depth_share, groups, col_count, tile_size), col_id, 1, 2
        )
        gathered = lax.all_gather(own_pieces, ("row", "col"), axis=2, tiled=True)
        flat_tiles = gathered.reshape(depth_share, groups * row_count * col_count, tile_size)
        tile_group = global_cols // row_count
        tile_row = global_cols % row_count
        take_index = (
            tile_group // col_count * (row_count * col_count)
            + tile_row * col_count
            + tile_group % col_count
        )
        col_tiles = jnp.take(flat_tiles, take_index, axis=1)
        return (panel_rows, col_tiles)

    def place_panel(panel_rows):
        row_tiles = jnp.transpose(panel_rows, (1, 2, 0))
        empty_tiles = jnp.zeros((tile_rows, tile_size, tile_size), jnp.float32)
        return lax.dynamic_update_slice(empty_tiles, row_tiles, (0, 0, depth_id * depth_share))

    updates = jnp.zeros((tile_rows, tile_size, tile_cols, tile_size), jnp.float32)
    run_updates = updates
    first_panel = rank_panel(0, run_updates)
    run_updates = apply_update(
        run_updates, 0, first_panel[0], global_rows, first_panel[-1], global_cols, 0, tile_cols
    )
    second_panel = rank_panel(1, run_updates)
    run_updates = apply_update(
        run_updates, 1, second_panel[0], global_rows, second_panel[-1], global_cols, 0, tile_cols
    )
    first_rows = first_panel[0]
    second_rows = second_panel[0]
    updates = run_updates
    trailing = matrix * first_depth + updates
    result = jnp.where(
        is_first,
        place_panel(first_rows)[:, :, None, :],
        jnp.where(is_second, place_panel(second_rows)[:, :, None, :], trailing),
    )
    summed = lax.psum_scatter(result, "depth", scatter_dimension=0, tiled=True)
    return summed.reshape(tile_rows // depth_count, 1, tile_size, tile_cols, 1, tile_size)


def solution(mesh):
    in_specs = (P(None, "row", None, None, "col", None),)
    out_specs = P("depth", "row", None, None, "col", None)
    return jax.shard_map(shards, mesh=mesh, in_specs=in_specs, out_specs=out_specs, check_vma=False)
```

profile of v0, /device:TPU:100, one launch (start us, length us, event | category | flops | bytes accessed | tf_op | source)
XLA Modules:
  0.0 822.3 jit_solution(9116252360739108186)
XLA Ops:
  6.5 37.0 %copy.2 = f32[32,1,256,2,1,256]{2,5,3,0,4,1:T(8,128)} copy(f32[32,1,256,2,1,256]{5,4,3,2,1,0:T(1,128)} %param.14) | data formatting | bytes 33554432 | tf_op args[0]
  45.3 37.1 %copy.17 = f32[32,1,256,2,1,256]{2,5,0,3,1,4:T(8,128)} copy(f32[32,1,256,2,1,256]{5,4,3,2,1,0:T(1,128)} %param.14) | data formatting | bytes 33554432 | tf_op jit(solution)/shard_map/reshape | solution.py:47
  82.7 11.7 %cholesky.130 = f32[128,128]{1,0:T(8,128)S(1)} custom-call(f32[128,128]{1,0:T(8,128)S(1)} %cholesky.194), custom_call_target="Cholesky" | custom-call | tf_op jit(solution)/shard_map/jit(cholesky)/cholesky | solution.py:58
  94.4 9.8 %custom-call.13 = f32[1,128,128]{1,2,0:T(8,128)S(1)} custom-call(f32[1,128,128]{2,1,0:T(8,128)S(1)} %get-tuple-element.91), custom_call_target="InvertDiagBlocksLowerTriangular" | custom-call | tf_op jit(solution)/shard_map/jit(cholesky)/cholesky | solution.py:58
  104.8 11.7 %cholesky.147 = f32[128,128]{1,0:T(8,128)S(1)} custom-call(f32[128,128]{1,0:T(8,128)S(1)} %convolution_subtract_fusion.3), custom_call_target="Cholesky" | custom-call | tf_op jit(solution)/shard_map/jit(cholesky)/cholesky | solution.py:58
  118.5 3.8 while.8
  122.3 19.9 %custom-call.14 = f32[2,128,128]{1,2,0:T(8,128)S(1)} custom-call(f32[2,128,128]{2,1,0:T(8,128)S(1)} %get-tuple-element.62), custom_call_target="InvertDiagBlocksLowerTriangular" | custom-call | tf_op jit(solution)/shard_map/jit(_solve_triangular)/triangular_solve | solution.py:59
  143.3 8.2 fusion.3
  151.6 74.5 %all-reduce.9.cloned.1.call-done = f32[16,32,256]{2,0,1:T(8,128)} async-done(((f32[16,32,256]{2,0,1:T(8,128)}), f32[16,32,256]{2,0,1:T(8,128)}) %all-reduce.9.cloned.1.call-update) | async-done | bytes 524304 | tf_op jit(solution)/shard_map/psum | solution.py:11
  228.1 37.1 %all-gather.3.cloned.1.call-done = f32[16,4,16,256]{3,0,2,1:T(8,128)} async-done(((f32[16,4,1,256]{3,0,2,1:T(8,128)}), f32[16,4,16,256]{3,0,2,1:T(8,128)}) %all-gather.3.cloned.1.call-update) | async-done | bytes 1048592 | tf_op jit(solution)/shard_map/all_gather | solution.py:77
  265.2 1.8 gather_fusion
  267.0 15.2 %negate_multiply_fusion = f32[32,256,2,256]{1,3,2,0:T(8,128)S(1)} fusion(f32[2]{0:T(128)S(1)} %get-tuple-element.97, f32[16,32,256]{2,0,1:T(8,128)} %all-reduce.9.cloned.1.call-done, f32[32]{0:T(128)S(1)} %compare_convert_fusion.4, f32[2,16,256]{2,1,0:T(8,128)S(1)} %gather_fusion, pred[2]{0:T(512)(128)(4,1)S(1)} %get-tuple-element.96), kind=kOutput, calls=%fused_computation.7 | convolution fusion | flops 813834240 | bytes 17334410 | tf_op jit(solution)/shard_map/kau,kcv->aucv/dot_general | solution.py:19
  282.3 5.7 copy-done
  288.0 3.8 slice_bitcast_fusion
  291.8 149.5 %all-reduce.11.cloned.1.call-done = f32[32,256,256]{1,2,0:T(8,128)} async-done(((f32[32,256,256]{1,2,0:T(8,128)}), f32[32,256,256]{1,2,0:T(8,128)}) %all-reduce.11.cloned.1.call-update) | async-done | bytes 8388624 | tf_op jit(solution)/shard_map/psum | solution.py:68
  441.3 10.4 %fusion = f32[32,256,256]{1,2,0:T(8,128)} fusion(f32[32,256,256]{1,2,0:T(8,128)} %all-reduce.11.cloned.1.call-done, f32[32,256,2,256]{1,3,0,2:T(8,128)} %bitcast.118), kind=kLoop, calls=%fused_computation.10 | loop fusion | flops 2097152 | bytes 25165824 | tf_op jit(solution)/shard_map/add | solution.py:68
  451.7 1.7 fusion.9
  453.5 29.6 %all-reduce.13.cloned.1.call-done = f32[256,256]{0,1:T(8,128)} async-done(((f32[256,256]{0,1:T(8,128)}), f32[256,256]{0,1:T(8,128)}) %all-reduce.13.cloned.1.call-update) | async-done | bytes 262160 | tf_op jit(solution)/shard_map/psum | solution.py:11
  483.4 11.7 %cholesky.164 = f32[128,128]{1,0:T(8,128)S(1)} custom-call(f32[128,128]{1,0:T(8,128)S(1)} %cholesky.197), custom_call_target="Cholesky" | custom-call | tf_op jit(solution)/shard_map/jit(cholesky)/cholesky | solution.py:58
  495.1 9.8 %custom-call.15 = f32[1,128,128]{1,2,0:T(8,128)S(1)} custom-call(f32[1,128,128]{2,1,0:T(8,128)S(1)} %get-tuple-element.87), custom_call_target="InvertDiagBlocksLowerTriangular" | custom-call | tf_op jit(solution)/shard_map/jit(cholesky)/cholesky | solution.py:58
  505.4 11.7 %cholesky.181 = f32[128,128]{1,0:T(8,128)S(1)} custom-call(f32[128,128]{1,0:T(8,128)S(1)} %convolution_subtract_fusion.2), custom_call_target="Cholesky" | custom-call | tf_op jit(solution)/shard_map/jit(cholesky)/cholesky | solution.py:58
  519.9 4.3 while.9
  524.2 19.7 %custom-call.16 = f32[2,128,128]{1,2,0:T(8,128)S(1)} custom-call(f32[2,128,128]{2,1,0:T(8,128)S(1)} %get-tuple-element.63), custom_call_target="InvertDiagBlocksLowerTriangular" | custom-call | tf_op jit(solution)/shard_map/jit(_solve_triangular)/triangular_solve | solution.py:59
  544.9 8.2 fusion.4
  553.2 74.0 %all-reduce.15.cloned.1.call-done = f32[16,32,256]{2,0,1:T(8,128)} async-done(((f32[16,32,256]{2,0,1:T(8,128)}), f32[16,32,256]{2,0,1:T(8,128)}) %all-reduce.15.cloned.1.call-update) | async-done | bytes 524304 | tf_op jit(solution)/shard_map/psum | solution.py:11
  628.8 4.2 broadcast_in_dim.50.clone.1
  633.9 4.2 broadcast_in_dim.50.clone
  638.9 27.5 %all-gather.5.cloned.1.call-done = f32[16,4,16,256]{3,0,2,1:T(8,128)} async-done(((f32[16,4,1,256]{3,0,2,1:T(8,128)}), f32[16,4,16,256]{3,0,2,1:T(8,128)}) %all-gather.5.cloned.1.call-update) | async-done | bytes 1048592 | tf_op jit(solution)/shard_map/all_gather | solution.py:77
  666.4 1.8 gather_fusion.1
  668.2 28.3 %select_select_fusion = f32[32,256,2,256]{1,3,2,0:T(8,128)} fusion(f32[32,256,2,256]{1,3,2,0:T(8,128)} %copy-done, f32[2]{0:T(128)S(1)} %get-tuple-element.98, f32[]{:T(128)S(6)} %convert_element_type.59, f32[32,256,256]{1,2,0:T(8,128)} %bitcast_dynamic-update-slice_fusion.2, f32[32,256,256]{1,2,0:T(8,128)} %bitcast_dynamic-update-slice_fusion.3, ...), kind=kOutput, calls=%fused_computation.6 | convolution fusion | flops 834805760 | bytes 67666064 | tf_op jit(solution)/shard_map/kau,kcv->aucv/dot_general | solution.py:19
  696.6 114.8 %reduce-scatter.2.cloned.1.call-done = f32[2,256,2,256]{1,3,2,0:T(8,128)} async-done(((f32[32,256,2,256]{1,3,2,0:T(8,128)}), f32[2,256,2,256]{1,3,2,0:T(8,128)}) %reduce-scatter.2.cloned.1.call-update) | async-done | bytes 1048592 | tf_op jit(solution)/shard_map/reduce_scatter | solution.py:113
  811.4 3.6 copy.10
  (82 shorter events, 20.9 us)
Async XLA Ops:
  6.5 75.9 %all-reduce.7.cloned.1.call-start = ((), (), s32[]{:S(2)}) async-start(), calls=%async_computation.1 | async-start | bytes 524288 | tf_op jit(solution)/shard_map/psum | solution.py:11
  45.2 180.8 %all-reduce.9.cloned.1.call-start = ((), (), s32[]{:S(2)}) async-start(), calls=%async_computation.2 | async-start | bytes 1048576 | tf_op jit(solution)/shard_map/psum | solution.py:11
  151.5 113.7 %all-gather.3.cloned.1.call-start = ((), (), s32[]{:S(2)}) async-start(), calls=%async_computation.3 | async-start | bytes 1114112 | tf_op jit(solution)/shard_map/all_gather | solution.py:77
  227.6 213.7 %all-reduce.11.cloned.1.call-start = ((), (), s32[]{:S(2)}) async-start(), calls=%async_computation.4 | async-start | bytes 16777216 | tf_op jit(solution)/shard_map/psum | solution.py:68
  282.3 5.7 copy-start
  291.8 191.4 %all-reduce.13.cloned.1.call-start = ((), (), s32[]{:S(2)}) async-start(), calls=%async_computation.5 | async-start | bytes 524288 | tf_op jit(solution)/shard_map/psum | solution.py:11
  451.7 181.3 %copy-start.1 = (f32[16,32,256]{2,0,1:T(8,128)S(1)}, f32[16,32,256]{2,0,1:T(8,128)}, u32[]{:S(2)}) copy-start(f32[16,32,256]{2,0,1:T(8,128)} %all-reduce.9.cloned.1.call-done) | copy-start | bytes 1572868
  453.5 173.7 %all-reduce.15.cloned.1.call-start = ((), (), s32[]{:S(2)}) async-start(), calls=%async_computation.6 | async-start | bytes 1048576 | tf_op jit(solution)/shard_map/psum | solution.py:11
  553.1 113.3 %all-gather.5.cloned.1.call-start = ((), (), s32[]{:S(2)}) async-start(), calls=%async_computation.7 | async-start | bytes 1114112 | tf_op jit(solution)/shard_map/all_gather | solution.py:77
  627.2 10.9 %copy-start.2 = (f32[16,32,256]{2,0,1:T(8,128)S(1)}, f32[16,32,256]{2,0,1:T(8,128)}, u32[]{:S(2)}) copy-start(f32[16,32,256]{2,0,1:T(8,128)} %all-reduce.15.cloned.1.call-done) | copy-start | bytes 1572868
  628.7 182.7 %reduce-scatter.2.cloned.1.call-start = ((), (), s32[]{:S(2)}) async-start(), calls=%async_computation.8 | async-start | bytes 17825792 | tf_op jit(solution)/shard_map/reduce_scatter | solution.py:113
Sparse Core Ops, SparseCore 0:
  45.4 30.8 all-reduce.6
  151.6 74.4 all-reduce.8
  227.9 37.2 all-gather.2
  291.9 149.3 all-reduce.10
  453.6 29.4 all-reduce.12
  553.2 73.8 all-reduce.14
  629.1 37.2 all-gather.4
  696.7 114.6 reduce-scatter.1
where the time goes:
time: 834 us; the launch traced here: 822 us
  waiting for transfers between devices  507 us (61%)
  other arithmetic  122 us (15%)
  local copies, waits for them, and re-layouts  112 us (13%)
  matrix products  63 us (8%)
  between operations  16.8 us (2%)
    psum x4, waiting for transfers between devices, from_root(): return lax.psum(block, axis)  178 us
    psum x1, waiting for transfers between devices, rank_panel(): column = column + lax.psum(updates[:, :, local_col, :], 'depth')  149 us
    reduce_scatter x1, waiting for transfers between devices, shards(): summed = lax.psum_scatter(result, 'depth', scatter_dimension=0, tiled=True)  115 us
    another operation x13, other arithmetic, pivot_inverse(): factor = jnp.linalg.cholesky(pivot_block)  68.6 us
    all_gather x2, waiting for transfers between devices, rank_panel(): gathered = lax.all_gather(own_pieces, ('row', 'col'), axis=2, tiled=True)  64.6 us
    dot_general x2, matrix products, outer_update(): jnp.einsum('kau,kcv->aucv', lower_rows, col_tiles, precision=highest)  43.6 us
    unnamed x7, local copies, waits for them, and re-layouts  42.7 us
    another operation x5, other arithmetic, pivot_inverse(): return jax.scipy.linalg.solve_triangular(factor, identity, lower=True)  39.6 us
  transfers between devices with their start and end apart: 8, of which 7 were waited for; matrix products, arithmetic and copies ran while one was open for 6% of the time, Pallas kernels for 0%

commit v1 on v0

v1 whole, which is shorter than its diff:
```python
import jax
import jax.numpy as jnp
from jax import lax
from jax.experimental import pallas as pl
from jax.experimental.pallas import tpu as pltpu
from jax.sharding import PartitionSpec as P

NB = 256
STEP = 32
SUB = 8
LANES = 128
highest = lax.Precision.HIGHEST


def dot(a, b, ca=1, cb=0):
    return lax.dot_general(
        a, b, (((ca,), (cb,)), ((), ())), precision=highest, preferred_element_type=jnp.float32
    )


def tile_from(ref):
    rows = ref.shape[0] // 2
    return jnp.concatenate([ref[pl.ds(0, rows, stride=2), :], ref[pl.ds(1, rows, stride=2), :]], axis=1)


def wide_from(ref):
    rows = ref.shape[0] // 4
    return jnp.concatenate([ref[pl.ds(q, rows, stride=4), :] for q in range(4)], axis=1)


def factor_panel(panel):
    groups = STEP // SUB
    lo = [panel[SUB * g : SUB * (g + 1), :LANES] for g in range(groups)]
    hi = [panel[SUB * g : SUB * (g + 1), LANES:] for g in range(groups)]
    shape = (SUB, LANES)
    lane = lax.broadcasted_iota(jnp.int32, shape, 1)
    sub = lax.broadcasted_iota(jnp.int32, shape, 0)
    for q in range(groups):
        live = range(q, groups)
        cols = [
            {g: jnp.broadcast_to(lo[g][:, SUB * q + j : SUB * q + j + 1], shape) for g in live}
            for j in range(SUB)
        ]
        d = {(i, j): jnp.broadcast_to(cols[j][q][i : i + 1, :], shape) for j in range(SUB) for i in range(j, SUB)}
        scale, low = [], {}
        for j in range(SUB):
            p = d[j, j]
            s = lax.rsqrt(p)
            scale.append(s)
            for i in range(j + 1, SUB):
                low[i, j] = d[i, j] * s
            for k in range(j + 1, SUB):
                for i in range(k, SUB):
                    d[i, k] = d[i, k] - low[i, j] * low[k, j]
        for j in range(SUB):
            s = scale[j]
            at = lane == SUB * q + j
            m = {g: cols[j][g] * s for g in live}
            for k in range(j + 1, SUB):
                for g in live:
                    cols[k][g] = cols[k][g] - m[g] * low[k, j]
            m[q] = jnp.where(sub > j, m[q], 0.0)
            row_lo = jnp.broadcast_to(lo[q][j : j + 1, :], shape)
            row_hi = jnp.broadcast_to(hi[q][j : j + 1, :], shape)
            u_lo = jnp.where(at, 1.0, row_lo) * s
            u_hi = row_hi * s
            for g in live:
                clear = at & (sub > j) if g == q else at
                lo[g] = jnp.where(clear, 0.0, lo[g]) - m[g] * u_lo
                hi[g] = hi[g] - m[g] * u_hi
            lo[q] = jnp.where(sub == j, u_lo, lo[q])
            hi[q] = jnp.where(sub == j, u_hi, hi[q])
    for g in range(groups):
        lo[g] = jnp.where((lane < STEP) & (lane > sub + SUB * g), 0.0, lo[g])
    return jnp.concatenate(
        [jnp.concatenate([lo[g], hi[g]], axis=1) for g in range(groups)], axis=0
    )


def factor(work, prev):
    row_id = lax.broadcasted_iota(jnp.int32, (NB, NB), 0)
    lane_id = lax.broadcasted_iota(jnp.int32, (NB, NB), 1)
    panel_lane = lax.broadcasted_iota(jnp.int32, (STEP, NB), 1)
    prev[...] = jnp.zeros((STEP, NB), jnp.float32)

    def body(step, carry):
        start = pl.multiple_of(step * STEP, STEP)
        stop = start + STEP
        turn = lax.rem(NB - start, NB)
        last = prev[...]
        rolled = pltpu.roll(last, turn, axis=1)
        panel = pltpu.roll(work[pl.ds(start, STEP), :], turn, axis=1)
        panel = jnp.where((panel_lane >= NB - STEP) & (step > 0), 0.0, panel)
        panel = panel - dot(rolled[:, :STEP], rolled, 0, 0)
        panel = pltpu.roll(factor_panel(panel), start, axis=1)
        below = jnp.where(panel_lane >= stop, last, 0.0)
        spent = (row_id >= stop) & (lane_id >= start - STEP) & (lane_id < start)
        work[...] = jnp.where(spent, 0.0, work[...]) - dot(below, last, 0, 0)
        work[pl.ds(start, STEP), :] = panel
        prev[...] = panel
        return carry

    lax.fori_loop(0, NB // STEP, body, 0)
    return jnp.where(lane_id <= row_id, work[...], 0.0)


def tiles_from(gathered, k, out):
    for d in range(16):
        out[pl.ds(16 * d, 16), :] = tile_from(gathered.at[d, k])


def first_kernel(ids, gathered, inv_ref, work, prev):
    tiles_from(gathered, 0, work)
    inv_ref[...] = factor(work, prev)


def second_kernel(ids, gathered, inv0_ref, up_ref, inv_ref, work, prev):
    tiles_from(gathered, 1, work)
    up = dot(inv0_ref[...], work[...], 1, 1)
    up_ref[...] = up
    tiles_from(gathered, 2, work)
    work[...] = work[...] - dot(up, up, 0, 0)
    inv_ref[...] = factor(work, prev)


def last_kernel(ids, slab, own_rows, other_rows, x0, x1, inv0_ref, up_ref, inv1_ref, out_ref):
    row, col, depth = ids[0], ids[1], ids[2]
    rows_a, rows_b = wide_from(own_rows), wide_from(other_rows)
    rows0 = jnp.where(row == 0, rows_a, rows_b)
    rows1 = jnp.where(row == 0, rows_b, rows_a)
    row_id = lax.broadcasted_iota(jnp.int32, (2 * NB, NB), 0)
    tile_id = 4 * depth + 2 * (row_id // NB) + row
    inv0, up, inv1 = inv0_ref[...], up_ref[...], inv1_ref[...]
    p0 = dot(tile_from(x0), inv0, 1, 1)
    q0 = dot(inv0, rows0)
    b0 = jnp.where(tile_id > 0, p0, 0.0)
    p1 = jnp.where(tile_id >= 1, dot(tile_from(x1) - dot(b0, up), inv1, 1, 1), 0.0)
    q1 = dot(inv1, rows1 - dot(up, q0, 0, 0))
    b1 = jnp.where(tile_id > 1, p1, 0.0)
    change = dot(b0, q0) + dot(b1, q1)
    for q in range(4):
        piece = slab[pl.ds(q, 2 * NB, stride=4), :] - change[:, q * LANES : (q + 1) * LANES]
        if q < 2:
            lanes = slice(q * LANES, (q + 1) * LANES)
            piece = jnp.where(col == 0, p0[:, lanes], jnp.where(col == 1, p1[:, lanes], piece))
        out_ref[pl.ds(q, 2 * NB, stride=4), :] = piece


def whole(shape):
    return pl.BlockSpec(shape, lambda i, ids: (0,) * len(shape))


def call(kernel, ids, args, specs, outs, scratch, flops):
    return pl.pallas_call(
        kernel,
        out_shape=[jax.ShapeDtypeStruct(s, jnp.float32) for s in outs],
        grid_spec=pltpu.PrefetchScalarGridSpec(
            num_scalar_prefetch=1,
            grid=(1,),
            in_specs=specs,
            out_specs=[whole(s) for s in outs],
            scratch_shapes=[pltpu.VMEM(s, jnp.float32) for s in scratch],
        ),
        compiler_params=pltpu.CompilerParams(vmem_limit_bytes=32 * 1024 * 1024),
        cost_estimate=pl.CostEstimate(flops=flops, bytes_accessed=1 << 20, transcendentals=0),
    )(ids, *args)


def choose(col, table):
    out = table[0][0]
    for value, cols in table[1:]:
        for c in cols:
            out = jnp.where(col == c, value, out)
    return out


def shards(gram_slab):
    row = lax.axis_index("row")
    col = lax.axis_index("col")
    depth = lax.axis_index("depth")
    ids = jnp.stack([row, col, depth]).astype(jnp.int32)
    flat = gram_slab.reshape(32 * NB * 4, LANES)

    def swap(x):
        return lax.ppermute(x, "row", [(0, 1), (1, 0)])

    def send(x, pairs):
        return lax.ppermute(x, "col", pairs)

    def to_all(x, axis, size):
        return lax.all_to_all(jnp.broadcast_to(x[None], (size, *x.shape)), axis, 0, 0, tiled=True)

    tile = lax.dynamic_slice_in_dim(flat, depth * 64, 64, 0).reshape(16, 4, LANES)[:, :2]
    mine = to_all(tile.reshape(32, LANES), "col", 8)[:2]
    block = lax.dynamic_slice_in_dim(flat, depth * 2048, 2048, 0)
    strip = block.reshape(512, 4, LANES)[:, :2].reshape(1024, LANES)
    strip, mine = lax.optimization_barrier((strip, mine))
    x_a = send(strip, [(0, 3), (1, 4)])
    x_b = send(strip, [(0, 5), (1, 6)])
    other = swap(mine)
    upper, lower = jnp.where(row == 0, mine, other), jnp.where(row == 0, other, mine)
    gathered = to_all(jnp.stack([upper[0], lower[0], lower[1]]), "depth", 16)

    square = whole((NB, NB))
    scratch = [(NB, NB), (STEP, NB)]
    pieces = whole(gathered.shape)
    (inv0,) = call(first_kernel, ids, (gathered,), [pieces], [(NB, NB)], scratch, 10**10)
    x_a, x_b, inv0 = lax.optimization_barrier((x_a, x_b, inv0))
    held = choose(col, [(strip, ()), (x_a, (3, 4)), (x_b, (5, 6))])
    x_c = send(held, [(0, 1), (3, 4), (5, 6), (1, 2), (4, 5), (6, 7)])
    x_d = send(held, [(0, 7), (3, 2), (1, 0), (4, 3)])
    up, inv1 = call(
        second_kernel, ids, (gathered, inv0), [pieces, square], [(NB, NB)] * 2, scratch, 10**10
    )
    x0 = choose(col, [(held, ()), (x_c, (1, 4, 6)), (x_d, (2, 7))])
    x1 = choose(col, [(held, ()), (x_c, (2, 5, 7)), (x_d, (0, 3))])
    own_rows = flat[: NB * 4]
    other_rows = swap(own_rows)
    (out,) = call(
        last_kernel,
        ids,
        (block, own_rows, other_rows, x0, x1, inv0, up, inv1),
        [whole((2048, LANES))] + [whole((1024, LANES))] * 4 + [square] * 3,
        [(2048, LANES)],
        [],
        10**9,
    )
    return out.reshape(2, 1, NB, 2, 1, NB)


def solution(mesh):
    in_specs = (P(None, "row", None, None, "col", None),)
    out_specs = P("depth", "row", None, None, "col", None)
    return jax.shard_map(shards, mesh=mesh, in_specs=in_specs, out_specs=out_specs, check_vma=False)
```

time: 834 us -> 85.5 us (0.10)
  the two profiles are of different devices: /device:TPU:100 before, /device:TPU:2 now
where the time goes in v1:
time: 85.5 us; the launch traced here: 85 us
  Pallas kernels  31.3 us (37%)
  starting transfers between devices  27.2 us (32%)
  waiting for transfers between devices  19.5 us (23%)
  local copies, waits for them, and re-layouts  5.28 us (6%)
  other arithmetic  1.54 us (2%)
    pallas_call x3, Pallas kernels, call(): pl.pallas_call(kernel, out_shape=[jax.ShapeDtypeStruct(s, jnp.float32) fo...  31.3 us
    all_to_all x2, starting transfers between devices, to_all(): lax.all_to_all(jnp.broadcast_to(x[None], (size, *x.shape)), axis, 0, 0, t...  15.9 us
    all_to_all x2, waiting for transfers between devices, to_all(): lax.all_to_all(jnp.broadcast_to(x[None], (size, *x.shape)), axis, 0, 0, t...  14.1 us
    ppermute x4, starting transfers between devices, send(): return lax.ppermute(x, 'col', pairs)  11.2 us
    ppermute x4, waiting for transfers between devices, send(): return lax.ppermute(x, 'col', pairs)  4.21 us
  transfers between devices with their start and end apart: 8, of which 4 were waited for; matrix products, arithmetic and copies ran while one was open for 5% of the time, Pallas kernels for 29%

profile of v1, /device:TPU:2, one launch (start us, length us, event | category | flops | bytes accessed | tf_op | source)
XLA Modules:
  0.0 85.0 jit_solution(10274092030316379978)
XLA Ops:
  0.0 0.8 constant_dynamic-slice_fusion
  0.8 0.7 broadcast_in_dim.14
  1.4 8.5 %all-to-all-start = ((f32[8,32,128]{2,1,0:T(8,128)}), f32[8,32,128]{2,1,0:T(8,128)S(1)}, u32[]{:S(2)}, u32[]{:S(2)}) async-start(f32[8,32,128]{2,1,0:T(8,128)} %broadcast_in_dim.14), calls=%async_computation | async-start | bytes 262144 | tf_op jit(solution)/shard_map/all_to_all | solution.py:191
  9.9 1.3 %constant_dynamic-slice_fusion.1.slab = f32[2048,128]{1,0:T(8,128)S(1)} fusion(f32[32768,128]{1,0:T(8,128)} %bitcast.17, s32[]{:T(128)S(6)} %select_n.92), kind=kLoop, calls=%fused_computation.11 | loop fusion | bytes 2097156 | tf_op jit(solution)/shard_map/dynamic_slice | solution.py:195
  11.2 0.2 slice.27
  11.4 7.6 %all-to-all-done = f32[8,32,128]{2,1,0:T(8,128)S(1)} async-done(((f32[8,32,128]{2,1,0:T(8,128)}), f32[8,32,128]{2,1,0:T(8,128)S(1)}, u32[]{:S(2)}, u32[]{:S(2)}) %all-to-all-start) | async-done | bytes 131104 | tf_op jit(solution)/shard_map/all_to_all | solution.py:191
  19.0 0.0 collective-permute-start.3
  19.0 1.2 %collective-permute-done.3 = f32[2,32,128]{2,1,0:T(8,128)S(1)} collective-permute-done((f32[2,32,128]{2,1,0:T(8,128)S(1)}, f32[2,32,128]{2,1,0:T(8,128)S(1)}, u32[]{:S(2)}, u32[]{:S(2)}) %collective-permute-start.3) | collective-permute-done | bytes 32800 | tf_op jit(solution)/shard_map/ppermute | solution.py:185
  20.2 1.0 %broadcast_in_dim.15 = f32[16,3,32,128]{3,2,1,0:T(8,128)} broadcast(f32[3,32,128]{2,1,0:T(8,128)S(1)} %pad_maximum_fusion), dimensions={1,2,3} | broadcast | bytes 835584 | tf_op jit(solution)/shard_map/broadcast_in_dim | solution.py:191
  21.2 7.5 %all-to-all-start.1 = ((f32[16,3,32,128]{3,2,1,0:T(8,128)}), f32[16,3,32,128]{3,2,1,0:T(8,128)S(1)}, u32[]{:S(2)}, u32[]{:S(2)}) async-start(f32[16,3,32,128]{3,2,1,0:T(8,128)} %broadcast_in_dim.15), calls=%async_computation.1 | async-start | bytes 1572864 | tf_op jit(solution)/shard_map/all_to_all | solution.py:191
  28.7 1.4 %slice.21 = f32[1,1,256,2,1,256]{5,4,3,2,1,0:T(1,128)S(1)} slice(f32[32,1,256,2,1,256]{5,4,3,2,1,0:T(1,128)} %param.1), slice={[0:1], [0:1], [0:256], [0:2], [0:1], [0:256]} | slice | bytes 1048576 | tf_op jit(solution)/shard_map/slice | solution.py:217
  30.1 0.1 collective-permute-start
  30.2 0.1 pad_add_fusion.ids
  30.3 3.2 %collective-permute-start.1 = (f32[1024,128]{1,0:T(8,128)S(1)}, f32[1024,128]{1,0:T(8,128)}, u32[]{:S(2)}, u32[]{:S(2)}) collective-permute-start(f32[1024,128]{1,0:T(8,128)S(1)} %bitcast.13), channel_id=1, source_target_pairs={{0,48},{16,64},{1,49},{17,65},{2,50},{18,66},{3,51},{19,67},{4,52}... | collective-permute-start | bytes 1572872 | tf_op jit(solution)/shard_map/ppermute | solution.py:188
  33.5 2.1 %collective-permute-start.2 = (f32[1024,128]{1,0:T(8,128)S(1)}, f32[1024,128]{1,0:T(8,128)}, u32[]{:S(2)}, u32[]{:S(2)}) collective-permute-start(f32[1024,128]{1,0:T(8,128)S(1)} %bitcast.14), channel_id=1, source_target_pairs={{0,80},{16,96},{1,81},{17,97},{2,82},{18,98},{3,83},{19,99},{4,84}... | collective-permute-start | bytes 1572872 | tf_op jit(solution)/shard_map/ppermute | solution.py:188
  35.6 6.4 %all-to-all-done.1.gathered = f32[16,3,32,128]{3,2,1,0:T(8,128)S(1)} async-done(((f32[16,3,32,128]{3,2,1,0:T(8,128)}), f32[16,3,32,128]{3,2,1,0:T(8,128)S(1)}, u32[]{:S(2)}, u32[]{:S(2)}) %all-to-all-start.1) | async-done | bytes 786464 | tf_op jit(solution)/shard_map/all_to_all | solution.py:191
  42.0 11.6 %shard_map.17.inv0_ref = f32[256,256]{1,0:T(8,128)S(1)} custom-call(s32[3]{0:T(128)S(1)} %pad_add_fusion.ids, f32[16,3,32,128]{3,2,1,0:T(8,128)S(1)} %all-to-all-done.1.gathered), custom_call_target="tpu_custom_call" | custom-call | flops 10000000000 | bytes 1048576 | tf_op jit(solution)/shard_map/pallas_call | solution.py:154
  53.6 0.0 collective-permute-done.1
  53.6 4.2 %collective-permute-done.2 = f32[1024,128]{1,0:T(8,128)} collective-permute-done((f32[1024,128]{1,0:T(8,128)S(1)}, f32[1024,128]{1,0:T(8,128)}, u32[]{:S(2)}, u32[]{:S(2)}) %collective-permute-start.2) | collective-permute-done | bytes 524320 | tf_op jit(solution)/shard_map/ppermute | solution.py:188
  57.9 1.3 %select_select_fusion.4 = f32[1024,128]{1,0:T(8,128)S(1)} fusion(f32[1024,128]{1,0:T(8,128)} %collective-permute-done.2, f32[1024,128]{1,0:T(8,128)} %collective-permute-done.1, f32[1024,128]{1,0:T(8,128)S(1)} %bitcast.15, pred[]{:T(512)S(6)} %eq.39, pred[]{:T(512)S(6)} %eq.38, pred[]{:T(512)S(6)} %eq.37, pred[]{:T(512)S(6)} %eq.35), kind=kLoop, calls=%fused_computation.4 | loop fusion | flops 524288 | bytes 2097156 | tf_op jit(solution)/shard_map/jit(_where)/select_n | solution.py:173
  59.1 1.9 %collective-permute-start.4 = (f32[1024,128]{1,0:T(8,128)S(1)}, f32[1024,128]{1,0:T(8,128)S(1)}, u32[]{:S(2)}, u32[]{:S(2)}) collective-permute-start(f32[1024,128]{1,0:T(8,128)S(1)} %select_select_fusion.4), channel_id=1, source_target_pairs={{0,112},{48,32},{16,0},{64,48},{1,113},{49,33},{17,1},{65,49},{2,1... | collective-permute-start | bytes 1572872 | tf_op jit(solution)/shard_map/ppermute | solution.py:188
  61.1 4.0 %collective-permute-start.5 = (f32[1024,128]{1,0:T(8,128)S(1)}, f32[1024,128]{1,0:T(8,128)S(1)}, u32[]{:S(2)}, u32[]{:S(2)}) collective-permute-start(f32[1024,128]{1,0:T(8,128)S(1)} %select_select_fusion.4), channel_id=1, source_target_pairs={{0,16},{48,64},{80,96},{16,32},{64,80},{96,112},{1,17},{49,65},{81... | collective-permute-start | bytes 1572872 | tf_op jit(solution)/shard_map/ppermute | solution.py:188
  65.0 12.7 %shard_map.18 = (f32[256,256]{1,0:T(8,128)S(1)}, f32[256,256]{1,0:T(8,128)S(1)}) custom-call(s32[3]{0:T(128)S(1)} %pad_add_fusion.ids, f32[16,3,32,128]{3,2,1,0:T(8,128)S(1)} %all-to-all-done.1.gathered, f32[256,256]{1,0:T(8,128)S(1)} %shard_map.17.inv0_ref), custom_call_target="tpu_custom_call" | custom-call | flops 10000000000 | bytes 1048576 | tf_op jit(solution)/shard_map/pallas_call | solution.py:154
  77.8 0.0 collective-permute-done.4
  77.8 0.0 collective-permute-done.5
  77.8 0.2 select_select_fusion
  78.0 0.0 collective-permute-done.other_rows
  78.0 7.0 %shard_map.19 = f32[2048,128]{1,0:T(8,128)} custom-call(s32[3]{0:T(128)S(1)} %pad_add_fusion.ids, f32[2048,128]{1,0:T(8,128)S(1)} %constant_dynamic-slice_fusion.1.slab, f32[1024,128]{1,0:T(8,128)S(1)} %bitcast.12, f32[1024,128]{1,0:T(8,128)S(1)} %collective-permute-done.other_rows, f32[1024,128]{1,0:T(8,128)S(1)} %get-tuple-element.20.x0, ...), custom_call_target="tpu_custom_call" | custom-call | flops 1000000000 | bytes 1048576 | tf_op jit(solution)/shard_map/pallas_call | solution.py:154
  (5 shorter events, 0.0 us)
Async XLA Ops:
  1.4 17.6 %all-to-all-start = ((f32[8,32,128]{2,1,0:T(8,128)}), f32[8,32,128]{2,1,0:T(8,128)S(1)}, u32[]{:S(2)}, u32[]{:S(2)}) async-start(f32[8,32,128]{2,1,0:T(8,128)} %broadcast_in_dim.14), calls=%async_computation | async-start | bytes 262144 | tf_op jit(solution)/shard_map/all_to_all | solution.py:191
  19.0 1.2 %collective-permute-start.3 = (f32[2,32,128]{2,1,0:T(8,128)S(1)}, f32[2,32,128]{2,1,0:T(8,128)S(1)}, u32[]{:S(2)}, u32[]{:S(2)}) collective-permute-start(f32[2,32,128]{2,1,0:T(8,128)S(1)} %slice.29), channel_id=1, source_target_pairs={{0,128},{128,0},{1,129},{129,1},{2,130},{130,2},{3,131},{131,3},{4... | collective-permute-start | bytes 98312 | tf_op jit(solution)/shard_map/ppermute | solution.py:185
  21.2 20.8 %all-to-all-start.1 = ((f32[16,3,32,128]{3,2,1,0:T(8,128)}), f32[16,3,32,128]{3,2,1,0:T(8,128)S(1)}, u32[]{:S(2)}, u32[]{:S(2)}) async-start(f32[16,3,32,128]{3,2,1,0:T(8,128)} %broadcast_in_dim.15), calls=%async_computation.1 | async-start | bytes 1572864 | tf_op jit(solution)/shard_map/all_to_all | solution.py:191
  30.1 47.9 %collective-permute-start = (f32[1024,128]{1,0:T(8,128)S(1)}, f32[1024,128]{1,0:T(8,128)S(1)}, u32[]{:S(2)}, u32[]{:S(2)}) collective-permute-start(f32[1024,128]{1,0:T(8,128)S(1)} %bitcast.11), channel_id=1, source_target_pairs={{0,128},{128,0},{1,129},{129,1},{2,130},{130,2},{3,131},{131,3},{4... | collective-permute-start | bytes 1572872 | tf_op jit(solution)/shard_map/ppermute | solution.py:185
  30.3 23.3 %collective-permute-start.1 = (f32[1024,128]{1,0:T(8,128)S(1)}, f32[1024,128]{1,0:T(8,128)}, u32[]{:S(2)}, u32[]{:S(2)}) collective-permute-start(f32[1024,128]{1,0:T(8,128)S(1)} %bitcast.13), channel_id=1, source_target_pairs={{0,48},{16,64},{1,49},{17,65},{2,50},{18,66},{3,51},{19,67},{4,52}... | collective-permute-start | bytes 1572872 | tf_op jit(solution)/shard_map/ppermute | solution.py:188
  33.5 24.3 %collective-permute-start.2 = (f32[1024,128]{1,0:T(8,128)S(1)}, f32[1024,128]{1,0:T(8,128)}, u32[]{:S(2)}, u32[]{:S(2)}) collective-permute-start(f32[1024,128]{1,0:T(8,128)S(1)} %bitcast.14), channel_id=1, source_target_pairs={{0,80},{16,96},{1,81},{17,97},{2,82},{18,98},{3,83},{19,99},{4,84}... | collective-permute-start | bytes 1572872 | tf_op jit(solution)/shard_map/ppermute | solution.py:188
  59.1 18.7 %collective-permute-start.4 = (f32[1024,128]{1,0:T(8,128)S(1)}, f32[1024,128]{1,0:T(8,128)S(1)}, u32[]{:S(2)}, u32[]{:S(2)}) collective-permute-start(f32[1024,128]{1,0:T(8,128)S(1)} %select_select_fusion.4), channel_id=1, source_target_pairs={{0,112},{48,32},{16,0},{64,48},{1,113},{49,33},{17,1},{65,49},{2,1... | collective-permute-start | bytes 1572872 | tf_op jit(solution)/shard_map/ppermute | solution.py:188
  61.1 16.7 %collective-permute-start.5 = (f32[1024,128]{1,0:T(8,128)S(1)}, f32[1024,128]{1,0:T(8,128)S(1)}, u32[]{:S(2)}, u32[]{:S(2)}) collective-permute-start(f32[1024,128]{1,0:T(8,128)S(1)} %select_select_fusion.4), channel_id=1, source_target_pairs={{0,16},{48,64},{80,96},{16,32},{64,80},{96,112},{1,17},{49,65},{81... | collective-permute-start | bytes 1572872 | tf_op jit(solution)/shard_map/ppermute | solution.py:188

commit v2 on v1

--- a/solution.py
+++ b/solution.py
@@ -15,6 +15,24 @@
 def dot(a, b, ca=1, cb=0):
     return lax.dot_general(
         a, b, (((ca,), (cb,)), ((), ())), precision=highest, preferred_element_type=jnp.float32
+    )
+
+
+def thin_dot(a, b):
+    def parts(x):
+        first = x.astype(jnp.bfloat16)
+        x = x - first.astype(jnp.float32)
+        second = x.astype(jnp.bfloat16)
+        third = (x - second.astype(jnp.float32)).astype(jnp.bfloat16)
+        return first, second, third
+
+    a1, a2, a3 = parts(a)
+    b1, b2, b3 = parts(b)
+    return lax.dot_general(
+        jnp.concatenate([a1, a1, a2, a1, a2, a3], axis=0),
+        jnp.concatenate([b1, b2, b1, b3, b2, b1], axis=0),
+        (((0,), (0,)), ((), ())),
+        preferred_element_type=jnp.float32,
     )
 
 
@@ -42,34 +60,44 @@
             for j in range(SUB)
         ]
         d = {(i, j): jnp.broadcast_to(cols[j][q][i : i + 1, :], shape) for j in range(SUB) for i in range(j, SUB)}
-        scale, low = [], {}
+        scale, low, inv = [], {}, {}
         for j in range(SUB):
-            p = d[j, j]
-            s = lax.rsqrt(p)
+            s = lax.rsqrt(d[j, j])
             scale.append(s)
             for i in range(j + 1, SUB):
                 low[i, j] = d[i, j] * s
             for k in range(j + 1, SUB):
                 for i in range(k, SUB):
                     d[i, k] = d[i, k] - low[i, j] * low[k, j]
+            inv[j, j] = s
+            for k in range(j):
+                total = low[j, k] * inv[k, k]
+                for i in range(k + 1, j):
+                    total = total + low[j, i] * inv[i, k]
+                inv[j, k] = -(total * s)
+        block = (lane >= SUB * q) & (lane < SUB * (q + 1))
+        unit = jnp.where(lane == sub + SUB * q, 1.0, 0.0)
+        row_lo = jnp.where(block, unit, lo[q])
+        new_lo, new_hi = jnp.zeros(shape, jnp.float32), jnp.zeros(shape, jnp.float32)
         for j in range(SUB):
-            s = scale[j]
-            at = lane == SUB * q + j
-            m = {g: cols[j][g] * s for g in live}
-            for k in range(j + 1, SUB):
-                for g in live:
-                    cols[k][g] = cols[k][g] - m[g] * low[k, j]
-            m[q] = jnp.where(sub > j, m[q], 0.0)
-            row_lo = jnp.broadcast_to(lo[q][j : j + 1, :], shape)
-            row_hi = jnp.broadcast_to(hi[q][j : j + 1, :], shape)
-            u_lo = jnp.where(at, 1.0, row_lo) * s
-            u_hi = row_hi * s
-            for g in live:
-                clear = at & (sub > j) if g == q else at
-                lo[g] = jnp.where(clear, 0.0, lo[g]) - m[g] * u_lo
-                hi[g] = hi[g] - m[g] * u_hi
-            lo[q] = jnp.where(sub == j, u_lo, lo[q])
-            hi[q] = jnp.where(sub == j, u_hi, hi[q])
+            weight = jnp.zeros(shape, jnp.float32)
+            for i in range(j, SUB):
+                weight = jnp.where(sub == i, inv[i, j], weight)
+            new_lo = new_lo + weight * jnp.broadcast_to(row_lo[j : j + 1, :], shape)
+            new_hi = new_hi + weight * jnp.broadcast_to(hi[q][j : j + 1, :], shape)
+        lo[q], hi[q] = new_lo, new_hi
+        below = range(q + 1, groups)
+        for g in below:
+            lo[g] = jnp.where(block, 0.0, lo[g])
+        for j in range(SUB):
+            u_lo = jnp.broadcast_to(lo[q][j : j + 1, :], shape)
+            u_hi = jnp.broadcast_to(hi[q][j : j + 1, :], shape)
+            for g in below:
+                m = cols[j][g] * scale[j]
+                for k in range(j + 1, SUB):
+                    cols[k][g] = cols[k][g] - m * low[k, j]
+                lo[g] = lo[g] - m * u_lo
+                hi[g] = hi[g] - m * u_hi
     for g in range(groups):
         lo[g] = jnp.where((lane < STEP) & (lane > sub + SUB * g), 0.0, lo[g])
     return jnp.concatenate(
@@ -91,11 +119,11 @@
         rolled = pltpu.roll(last, turn, axis=1)
         panel = pltpu.roll(work[pl.ds(start, STEP), :], turn, axis=1)
         panel = jnp.where((panel_lane >= NB - STEP) & (step > 0), 0.0, panel)
-        panel = panel - dot(rolled[:, :STEP], rolled, 0, 0)
+        panel = panel - thin_dot(rolled[:, :STEP], rolled)
         panel = pltpu.roll(factor_panel(panel), start, axis=1)
         below = jnp.where(panel_lane >= stop, last, 0.0)
         spent = (row_id >= stop) & (lane_id >= start - STEP) & (lane_id < start)
-        work[...] = jnp.where(spent, 0.0, work[...]) - dot(below, last, 0, 0)
+        work[...] = jnp.where(spent, 0.0, work[...]) - thin_dot(below, last)
         work[pl.ds(start, STEP), :] = panel
         prev[...] = panel
         return carry
@@ -104,21 +132,33 @@
     return jnp.where(lane_id <= row_id, work[...], 0.0)
 
 
-def tiles_from(gathered, k, out):
-    for d in range(16):
-        out[pl.ds(16 * d, 16), :] = tile_from(gathered.at[d, k])
-
-
-def first_kernel(ids, gathered, inv_ref, work, prev):
-    tiles_from(gathered, 0, work)
-    inv_ref[...] = factor(work, prev)
-
-
-def second_kernel(ids, gathered, inv0_ref, up_ref, inv_ref, work, prev):
-    tiles_from(gathered, 1, work)
+def tiles_from(ids, pieces, k, out):
+    y = ids[2] // 4
+    for j in range(4):
+        at = pl.multiple_of(lax.rem(y - j + 4, 4) * 64, 64)
+        out[pl.ds(at, 64), :] = tile_from(pieces[j].at[k])
+
+
+def first_tile(ref):
+    return jnp.concatenate([ref[pl.ds(q, NB, stride=4), :] for q in range(2)], axis=1)
+
+
+def first_kernel(ids, rows, out_ref, work, prev):
+    @pl.when((ids[0] == 0) & (ids[1] == 0))
+    def _():
+        work[...] = first_tile(rows)
+        inv = factor(work, prev)
+        for q in range(2):
+            out_ref[pl.ds(q, NB, stride=2), :] = inv[:, q * LANES : (q + 1) * LANES]
+
+
+def second_kernel(ids, a, b, c, d, inv0_ref, up_ref, inv_ref, work, prev):
+    pieces = (a, b, c, d)
+    tiles_from(ids, pieces, 0, inv0_ref)
+    tiles_from(ids, pieces, 1, work)
     up = dot(inv0_ref[...], work[...], 1, 1)
     up_ref[...] = up
-    tiles_from(gathered, 2, work)
+    tiles_from(ids, pieces, 2, work)
     work[...] = work[...] - dot(up, up, 0, 0)
     inv_ref[...] = factor(work, prev)
 
@@ -161,7 +201,7 @@
             out_specs=[whole(s) for s in outs],
             scratch_shapes=[pltpu.VMEM(s, jnp.float32) for s in scratch],
         ),
-        compiler_params=pltpu.CompilerParams(vmem_limit_bytes=32 * 1024 * 1024),
+        compiler_params=pltpu.CompilerParams(vmem_limit_bytes=40 * 1024 * 1024),
         cost_estimate=pl.CostEstimate(flops=flops, bytes_accessed=1 << 20, transcendentals=0),
     )(ids, *args)
 
@@ -187,35 +227,56 @@
     def send(x, pairs):
         return lax.ppermute(x, "col", pairs)
 
-    def to_all(x, axis, size):
-        return lax.all_to_all(jnp.broadcast_to(x[None], (size, *x.shape)), axis, 0, 0, tiled=True)
-
-    tile = lax.dynamic_slice_in_dim(flat, depth * 64, 64, 0).reshape(16, 4, LANES)[:, :2]
-    mine = to_all(tile.reshape(32, LANES), "col", 8)[:2]
+    def far(x):
+        return send(x, [(0, 3), (1, 4)]), send(x, [(0, 5), (1, 6)])
+
+    def near(x):
+        ahead = [(0, 1), (3, 4), (5, 6), (1, 2), (4, 5), (6, 7)]
+        return send(x, ahead), send(x, [(0, 7), (3, 2), (1, 0), (4, 3)])
+
+    def held_of(x, ahead, back):
+        return choose(col, [(x, ()), (ahead, (3, 4)), (back, (5, 6))])
+
+    def both_of(x, ahead, back):
+        return (
+            choose(col, [(x, ()), (ahead, (1, 4, 6)), (back, (2, 7))]),
+            choose(col, [(x, ()), (ahead, (2, 5, 7)), (back, (0, 3))]),
+        )
+
+    square = whole((NB, NB))
+    scratch = [(NB, NB), (STEP, NB)]
+    first_rows = pl.BlockSpec((1024, LANES), lambda i, ids: (0, 0))
+    (inv0,) = call(first_kernel, ids, (flat,), [first_rows], [(512, LANES)], scratch, 10**10)
+
     block = lax.dynamic_slice_in_dim(flat, depth * 2048, 2048, 0)
     strip = block.reshape(512, 4, LANES)[:, :2].reshape(1024, LANES)
-    strip, mine = lax.optimization_barrier((strip, mine))
-    x_a = send(strip, [(0, 3), (1, 4)])
-    x_b = send(strip, [(0, 5), (1, 6)])
+    y = depth // 4
+    tile = lax.dynamic_slice_in_dim(flat, y * 256, 256, 0).reshape(64, 4, LANES)[:, :2]
+    inv0 = lax.dynamic_slice_in_dim(inv0, y * 128, 128, 0)
+    tile = jnp.where((row == 0) & (col == 0), inv0, tile.reshape(128, LANES))
+    x_a = send(strip, [(0, 5), (1, 4)])
+    x_b = send(strip, [(0, 1), (1, 0)])
+    tile = held_of(tile, *far(tile))
+    tile, x_a, x_b = lax.optimization_barrier((tile, x_a, x_b))
+    mine = jnp.stack(both_of(tile, *near(tile)))
+    x_c = send(choose(col, [(x_a, ()), (x_b, (1,))]), [(1, 2), (5, 4), (4, 3)])
+    x_d = send(choose(col, [(x_a, ()), (x_b, (0,))]), [(5, 6), (4, 5), (0, 7)])
     other = swap(mine)
     upper, lower = jnp.where(row == 0, mine, other), jnp.where(row == 0, other, mine)
-    gathered = to_all(jnp.stack([upper[0], lower[0], lower[1]]), "depth", 16)
-
-    square = whole((NB, NB))
-    scratch = [(NB, NB), (STEP, NB)]
-    pieces = whole(gathered.shape)
-    (inv0,) = call(first_kernel, ids, (gathered,), [pieces], [(NB, NB)], scratch, 10**10)
-    x_a, x_b, inv0 = lax.optimization_barrier((x_a, x_b, inv0))
-    held = choose(col, [(strip, ()), (x_a, (3, 4)), (x_b, (5, 6))])
-    x_c = send(held, [(0, 1), (3, 4), (5, 6), (1, 2), (4, 5), (6, 7)])
-    x_d = send(held, [(0, 7), (3, 2), (1, 0), (4, 3)])
-    up, inv1 = call(
-        second_kernel, ids, (gathered, inv0), [pieces, square], [(NB, NB)] * 2, scratch, 10**10
-    )
-    x0 = choose(col, [(held, ()), (x_c, (1, 4, 6)), (x_d, (2, 7))])
-    x1 = choose(col, [(held, ()), (x_c, (2, 5, 7)), (x_d, (0, 3))])
-    own_rows = flat[: NB * 4]
+    tiles = jnp.stack([upper[0], lower[0], lower[1]])
+    pieces = [tiles] + [
+        lax.ppermute(tiles, "depth", [(d, (d + 4 * j) % 16) for d in range(16)]) for j in (1, 2, 3)
+    ]
+
+    x_c, x_d, own_rows, *pieces = lax.optimization_barrier((x_c, x_d, flat[: NB * 4], *pieces))
     other_rows = swap(own_rows)
+    x_e = send(choose(col, [(x_c, ()), (x_d, (5, 6))]), [(4, 3), (6, 7), (3, 2), (5, 6)])
+    inv0, up, inv1 = call(
+        second_kernel, ids, pieces, [whole(tiles.shape)] * 4, [(NB, NB)] * 3, scratch, 10**10
+    )
+    x_e, inv1 = lax.optimization_barrier((x_e, inv1))
+    x0 = choose(col, [(x_e, ()), (strip, (0,)), (x_b, (1,)), (x_c, (2, 4)), (x_a, (5,)), (x_d, (6,))])
+    x1 = choose(col, [(x_e, ()), (x_b, (0,)), (strip, (1,)), (x_c, (3,)), (x_a, (4,)), (x_d, (5, 7))])
     (out,) = call(
         last_kernel,
         ids,

time: 85.5 us -> 79.2 us (0.926)
  the two profiles are of different devices: /device:TPU:2 before, /device:TPU:100 now
where the time goes in v2:
time: 79.2 us; the launch traced here: 78.9 us
  waiting for transfers between devices  38.2 us (48%)
  Pallas kernels  20.5 us (26%)
  starting transfers between devices  15.5 us (20%)
  local copies, waits for them, and re-layouts  3.82 us (5%)
    ppermute x9, waiting for transfers between devices, send(): return lax.ppermute(x, 'col', pairs)  28.5 us
    pallas_call x3, Pallas kernels, call(): pl.pallas_call(kernel, out_shape=[jax.ShapeDtypeStruct(s, jnp.float32) fo...  20.5 us
    ppermute x9, starting transfers between devices, send(): return lax.ppermute(x, 'col', pairs)  10.5 us
    ppermute x3, waiting for transfers between devices, shards(): lax.ppermute(tiles, 'depth', [(d, (d + 4 * j) % 16) for d in range(16)])  9.73 us
    ppermute x3, starting transfers between devices, shards(): lax.ppermute(tiles, 'depth', [(d, (d + 4 * j) % 16) for d in range(16)])  4.69 us
  transfers between devices with their start and end apart: 14, of which 7 were waited for; matrix products, arithmetic and copies ran while one was open for 4% of the time, Pallas kernels for 17%

profile of v2, /device:TPU:100, one launch (start us, length us, event | category | flops | bytes accessed | tf_op | source)
XLA Modules:
  0.0 78.9 jit_solution(14798648983091843523)
XLA Ops:
  0.0 1.3 %constant_dynamic-slice_fusion.1.slab = f32[2048,128]{1,0:T(8,128)S(1)} fusion(f32[32768,128]{1,0:T(8,128)} %bitcast.22, s32[]{:T(128)S(6)} %select_n.188), kind=kLoop, calls=%fused_computation.24 | loop fusion | bytes 2097156 | tf_op jit(solution)/shard_map/dynamic_slice | solution.py:251
  1.3 0.2 slice.24
  1.5 0.7 collective-permute-start.3
  2.2 0.7 collective-permute-start.2
  2.9 0.9 %constant_dynamic-slice_fusion = f32[256,128]{1,0:T(8,128)S(1)} fusion(f32[32768,128]{1,0:T(8,128)} %bitcast.23, s32[]{:T(128)S(6)} %select_n.194), kind=kLoop, calls=%fused_computation.23 | loop fusion | bytes 262148 | tf_op jit(solution)/shard_map/dynamic_slice | solution.py:254
  3.8 0.1 pad_add_fusion.ids
  3.9 1.6 %shard_map.17 = f32[512,128]{1,0:T(8,128)S(1)} custom-call(s32[3]{0:T(128)S(1)} %pad_add_fusion.ids, f32[32768,128]{1,0:T(8,128)} %bitcast.24), custom_call_target="tpu_custom_call" | custom-call | flops 10000000000 | bytes 1048576 | tf_op jit(solution)/shard_map/pallas_call | solution.py:194
  5.6 1.3 %collective-permute-start.1 = (f32[128,128]{1,0:T(8,128)S(1)}, f32[128,128]{1,0:T(8,128)S(1)}, u32[]{:S(2)}, u32[]{:S(2)}) collective-permute-start(f32[128,128]{1,0:T(8,128)S(1)} %dynamic-slice_select_fusion), channel_id=1, source_target_pairs={{0,48},{16,64},{1,49},{17,65},{2,50},{18,66},{3,51},{19,67},{4,52}... | collective-permute-start | bytes 196616 | tf_op jit(solution)/shard_map/ppermute | solution.py:228
  6.9 0.7 collective-permute-start
  7.5 19.4 %collective-permute-done.1 = f32[128,128]{1,0:T(8,128)S(1)} collective-permute-done((f32[128,128]{1,0:T(8,128)S(1)}, f32[128,128]{1,0:T(8,128)S(1)}, u32[]{:S(2)}, u32[]{:S(2)}) %collective-permute-start.1) | collective-permute-done | bytes 65568 | tf_op jit(solution)/shard_map/ppermute | solution.py:228
  27.0 1.3 %collective-permute-start.7 = (f32[128,128]{1,0:T(8,128)S(1)}, f32[128,128]{1,0:T(8,128)S(1)}, u32[]{:S(2)}, u32[]{:S(2)}) collective-permute-start(f32[128,128]{1,0:T(8,128)S(1)} %select_select_fusion.7), channel_id=1, source_target_pairs={{0,16},{48,64},{80,96},{16,32},{64,80},{96,112},{1,17},{49,65},{81... | collective-permute-start | bytes 196616 | tf_op jit(solution)/shard_map/ppermute | solution.py:228
  28.3 1.9 %collective-permute-start.6 = (f32[128,128]{1,0:T(8,128)S(1)}, f32[128,128]{1,0:T(8,128)S(1)}, u32[]{:S(2)}, u32[]{:S(2)}) collective-permute-start(f32[128,128]{1,0:T(8,128)S(1)} %select_select_fusion.7), channel_id=1, source_target_pairs={{0,112},{48,32},{16,0},{64,48},{1,113},{49,33},{17,1},{65,49},{2,1... | collective-permute-start | bytes 196616 | tf_op jit(solution)/shard_map/ppermute | solution.py:228
  30.2 6.1 %collective-permute-done.6 = f32[128,128]{1,0:T(8,128)S(1)} collective-permute-done((f32[128,128]{1,0:T(8,128)S(1)}, f32[128,128]{1,0:T(8,128)S(1)}, u32[]{:S(2)}, u32[]{:S(2)}) %collective-permute-start.6) | collective-permute-done | bytes 65568 | tf_op jit(solution)/shard_map/ppermute | solution.py:228
  36.4 0.1 collective-permute-start.8
  36.5 0.1 broadcast_select_fusion
  36.6 0.7 collective-permute-start.5
  37.3 1.3 %collective-permute-start.4 = (f32[1024,128]{1,0:T(8,128)S(1)}, f32[1024,128]{1,0:T(8,128)S(1)}, u32[]{:S(2)}, u32[]{:S(2)}) collective-permute-start(f32[1024,128]{1,0:T(8,128)S(1)} %get-tuple-element.38), channel_id=1, source_target_pairs={{16,32},{80,64},{64,48},{17,33},{81,65},{65,49},{18,34},{82,66},{6... | collective-permute-start | bytes 1572872 | tf_op jit(solution)/shard_map/ppermute | solution.py:228
  38.7 3.1 %collective-permute-start.11 = (f32[3,128,128]{2,1,0:T(8,128)S(1)}, f32[3,128,128]{2,1,0:T(8,128)S(1)}, u32[]{:S(2)}, u32[]{:S(2)}) collective-permute-start(f32[3,128,128]{2,1,0:T(8,128)S(1)} %pad_maximum_fusion.a), channel_id=1, source_target_pairs={{0,12},{1,13},{2,14},{3,15},{4,0},{5,1},{6,2},{7,3},{8,4},{9,5},{1... | collective-permute-start | bytes 589832 | tf_op jit(solution)/shard_map/ppermute | solution.py:268
  41.8 0.6 collective-permute-start.10
  42.4 1.0 %collective-permute-start.9 = (f32[3,128,128]{2,1,0:T(8,128)S(1)}, f32[3,128,128]{2,1,0:T(8,128)S(1)}, u32[]{:S(2)}, u32[]{:S(2)}) collective-permute-start(f32[3,128,128]{2,1,0:T(8,128)S(1)} %pad_maximum_fusion.a), channel_id=1, source_target_pairs={{0,4},{1,5},{2,6},{3,7},{4,8},{5,9},{6,10},{7,11},{8,12},{9,13},{1... | collective-permute-start | bytes 589832 | tf_op jit(solution)/shard_map/ppermute | solution.py:268
  43.4 1.4 %slice.20 = f32[1,1,256,2,1,256]{5,4,3,2,1,0:T(1,128)S(1)} slice(f32[32,1,256,2,1,256]{5,4,3,2,1,0:T(1,128)} %param.1), slice={[0:1], [0:1], [0:256], [0:2], [0:1], [0:256]} | slice | bytes 1048576 | tf_op jit(solution)/shard_map/slice | solution.py:271
  44.8 6.0 %collective-permute-done.11.d = f32[3,128,128]{2,1,0:T(8,128)S(1)} collective-permute-done((f32[3,128,128]{2,1,0:T(8,128)S(1)}, f32[3,128,128]{2,1,0:T(8,128)S(1)}, u32[]{:S(2)}, u32[]{:S(2)}) %collective-permute-start.11) | collective-permute-done | bytes 196640 | tf_op jit(solution)/shard_map/ppermute | solution.py:268
  50.8 0.3 collective-permute-done.10.c
  51.1 3.5 %collective-permute-done.9.b = f32[3,128,128]{2,1,0:T(8,128)S(1)} collective-permute-done((f32[3,128,128]{2,1,0:T(8,128)S(1)}, f32[3,128,128]{2,1,0:T(8,128)S(1)}, u32[]{:S(2)}, u32[]{:S(2)}) %collective-permute-start.9) | collective-permute-done | bytes 196640 | tf_op jit(solution)/shard_map/ppermute | solution.py:268
  54.5 0.2 collective-permute-done.4
  54.7 0.1 select_select_fusion.2
  54.8 1.9 %collective-permute-start.13 = (f32[1024,128]{1,0:T(8,128)S(1)}, f32[1024,128]{1,0:T(8,128)S(1)}, u32[]{:S(2)}, u32[]{:S(2)}) collective-permute-start(f32[1024,128]{1,0:T(8,128)S(1)} %select_select_fusion.2), channel_id=1, source_target_pairs={{64,48},{96,112},{48,32},{80,96},{65,49},{97,113},{49,33},{81,97},... | collective-permute-start | bytes 1572872 | tf_op jit(solution)/shard_map/ppermute | solution.py:228
  56.7 0.3 collective-permute-start.12
  57.0 11.8 %shard_map.18 = (f32[256,256]{1,0:T(8,128)S(1)}, f32[256,256]{1,0:T(8,128)S(1)}, f32[256,256]{1,0:T(8,128)S(1)}) custom-call(s32[3]{0:T(128)S(1)} %pad_add_fusion.ids, f32[3,128,128]{2,1,0:T(8,128)S(1)} %pad_maximum_fusion.a, f32[3,128,128]{2,1,0:T(8,128)S(1)} %collective-permute-done.9.b, f32[3,128,128]{2,1,0:T(8,128)S(1)} %collective-permute-done.10.c, ...), custom_call_target="tpu_custom_call" | custom-call | flops 10000000000 | bytes 1048576 | tf_op jit(solution)/shard_map/pallas_call | solution.py:194
  68.8 2.7 %collective-permute-done.13 = f32[1024,128]{1,0:T(8,128)S(1)} collective-permute-done((f32[1024,128]{1,0:T(8,128)S(1)}, f32[1024,128]{1,0:T(8,128)S(1)}, u32[]{:S(2)}, u32[]{:S(2)}) %collective-permute-start.13) | collective-permute-done | bytes 524320 | tf_op jit(solution)/shard_map/ppermute | solution.py:228
  71.5 0.3 select_select_fusion
  71.8 7.0 %shard_map.19 = f32[2048,128]{1,0:T(8,128)} custom-call(s32[3]{0:T(128)S(1)} %pad_add_fusion.ids, f32[2048,128]{1,0:T(8,128)S(1)} %constant_dynamic-slice_fusion.1.slab, f32[1024,128]{1,0:T(8,128)S(1)} %bitcast.16, f32[1024,128]{1,0:T(8,128)S(1)} %collective-permute-done.12.other_rows, f32[1024,128]{1,0:T(8,128)S(1)} %get-tuple-element.36.x0, ...), custom_call_target="tpu_custom_call" | custom-call | flops 1000000000 | bytes 1048576 | tf_op jit(solution)/shard_map/pallas_call | solution.py:194
  (15 shorter events, 0.1 us)
Async XLA Ops:
  1.5 25.5 %collective-permute-start.3 = (f32[1024,128]{1,0:T(8,128)S(1)}, f32[1024,128]{1,0:T(8,128)S(1)}, u32[]{:S(2)}, u32[]{:S(2)}) collective-permute-start(f32[1024,128]{1,0:T(8,128)S(1)} %bitcast.17), channel_id=1, source_target_pairs={{0,16},{16,0},{1,17},{17,1},{2,18},{18,2},{3,19},{19,3},{4,20},{20... | collective-permute-start | bytes 1572872 | tf_op jit(solution)/shard_map/ppermute | solution.py:228
  2.2 24.8 %collective-permute-start.2 = (f32[1024,128]{1,0:T(8,128)S(1)}, f32[1024,128]{1,0:T(8,128)S(1)}, u32[]{:S(2)}, u32[]{:S(2)}) collective-permute-start(f32[1024,128]{1,0:T(8,128)S(1)} %bitcast.18), channel_id=1, source_target_pairs={{0,80},{16,64},{1,81},{17,65},{2,82},{18,66},{3,83},{19,67},{4,84}... | collective-permute-start | bytes 1572872 | tf_op jit(solution)/shard_map/ppermute | solution.py:228
  5.6 21.4 %collective-permute-start.1 = (f32[128,128]{1,0:T(8,128)S(1)}, f32[128,128]{1,0:T(8,128)S(1)}, u32[]{:S(2)}, u32[]{:S(2)}) collective-permute-start(f32[128,128]{1,0:T(8,128)S(1)} %dynamic-slice_select_fusion), channel_id=1, source_target_pairs={{0,48},{16,64},{1,49},{17,65},{2,50},{18,66},{3,51},{19,67},{4,52}... | collective-permute-start | bytes 196616 | tf_op jit(solution)/shard_map/ppermute | solution.py:228
  6.9 20.1 %collective-permute-start = (f32[128,128]{1,0:T(8,128)S(1)}, f32[128,128]{1,0:T(8,128)S(1)}, u32[]{:S(2)}, u32[]{:S(2)}) collective-permute-start(f32[128,128]{1,0:T(8,128)S(1)} %dynamic-slice_select_fusion), channel_id=1, source_target_pairs={{0,80},{16,96},{1,81},{17,97},{2,82},{18,98},{3,83},{19,99},{4,84}... | collective-permute-start | bytes 196616 | tf_op jit(solution)/shard_map/ppermute | solution.py:228
  27.0 3.2 %collective-permute-start.7 = (f32[128,128]{1,0:T(8,128)S(1)}, f32[128,128]{1,0:T(8,128)S(1)}, u32[]{:S(2)}, u32[]{:S(2)}) collective-permute-start(f32[128,128]{1,0:T(8,128)S(1)} %select_select_fusion.7), channel_id=1, source_target_pairs={{0,16},{48,64},{80,96},{16,32},{64,80},{96,112},{1,17},{49,65},{81... | collective-permute-start | bytes 196616 | tf_op jit(solution)/shard_map/ppermute | solution.py:228
  28.3 8.1 %collective-permute-start.6 = (f32[128,128]{1,0:T(8,128)S(1)}, f32[128,128]{1,0:T(8,128)S(1)}, u32[]{:S(2)}, u32[]{:S(2)}) collective-permute-start(f32[128,128]{1,0:T(8,128)S(1)} %select_select_fusion.7), channel_id=1, source_target_pairs={{0,112},{48,32},{16,0},{64,48},{1,113},{49,33},{17,1},{65,49},{2,1... | collective-permute-start | bytes 196616 | tf_op jit(solution)/shard_map/ppermute | solution.py:228
  36.4 2.2 %collective-permute-start.8 = (f32[2,128,128]{2,1,0:T(8,128)S(1)}, f32[2,128,128]{2,1,0:T(8,128)S(1)}, u32[]{:S(2)}, u32[]{:S(2)}) collective-permute-start(f32[2,128,128]{2,1,0:T(8,128)S(1)} %pad_maximum_fusion.1), channel_id=1, source_target_pairs={{0,128},{128,0},{1,129},{129,1},{2,130},{130,2},{3,131},{131,3},{4... | collective-permute-start | bytes 393224 | tf_op jit(solution)/shard_map/ppermute | solution.py:225
  36.6 17.9 %collective-permute-start.5 = (f32[1024,128]{1,0:T(8,128)S(1)}, f32[1024,128]{1,0:T(8,128)S(1)}, u32[]{:S(2)}, u32[]{:S(2)}) collective-permute-start(f32[1024,128]{1,0:T(8,128)S(1)} %get-tuple-element.37), channel_id=1, source_target_pairs={{80,96},{64,80},{0,112},{81,97},{65,81},{1,113},{82,98},{66,82},{2... | collective-permute-start | bytes 1572872 | tf_op jit(solution)/shard_map/ppermute | solution.py:228
  37.3 17.4 %collective-permute-start.4 = (f32[1024,128]{1,0:T(8,128)S(1)}, f32[1024,128]{1,0:T(8,128)S(1)}, u32[]{:S(2)}, u32[]{:S(2)}) collective-permute-start(f32[1024,128]{1,0:T(8,128)S(1)} %get-tuple-element.38), channel_id=1, source_target_pairs={{16,32},{80,64},{64,48},{17,33},{81,65},{65,49},{18,34},{82,66},{6... | collective-permute-start | bytes 1572872 | tf_op jit(solution)/shard_map/ppermute | solution.py:228
  38.7 12.1 %collective-permute-start.11 = (f32[3,128,128]{2,1,0:T(8,128)S(1)}, f32[3,128,128]{2,1,0:T(8,128)S(1)}, u32[]{:S(2)}, u32[]{:S(2)}) collective-permute-start(f32[3,128,128]{2,1,0:T(8,128)S(1)} %pad_maximum_fusion.a), channel_id=1, source_target_pairs={{0,12},{1,13},{2,14},{3,15},{4,0},{5,1},{6,2},{7,3},{8,4},{9,5},{1... | collective-permute-start | bytes 589832 | tf_op jit(solution)/shard_map/ppermute | solution.py:268
  41.8 9.3 %collective-permute-start.10 = (f32[3,128,128]{2,1,0:T(8,128)S(1)}, f32[3,128,128]{2,1,0:T(8,128)S(1)}, u32[]{:S(2)}, u32[]{:S(2)}) collective-permute-start(f32[3,128,128]{2,1,0:T(8,128)S(1)} %pad_maximum_fusion.a), channel_id=1, source_target_pairs={{0,8},{1,9},{2,10},{3,11},{4,12},{5,13},{6,14},{7,15},{8,0},{9,1},... | collective-permute-start | bytes 589832 | tf_op jit(solution)/shard_map/ppermute | solution.py:268
  42.4 12.1 %collective-permute-start.9 = (f32[3,128,128]{2,1,0:T(8,128)S(1)}, f32[3,128,128]{2,1,0:T(8,128)S(1)}, u32[]{:S(2)}, u32[]{:S(2)}) collective-permute-start(f32[3,128,128]{2,1,0:T(8,128)S(1)} %pad_maximum_fusion.a), channel_id=1, source_target_pairs={{0,4},{1,5},{2,6},{3,7},{4,8},{5,9},{6,10},{7,11},{8,12},{9,13},{1... | collective-permute-start | bytes 589832 | tf_op jit(solution)/shard_map/ppermute | solution.py:268
  54.8 16.7 %collective-permute-start.13 = (f32[1024,128]{1,0:T(8,128)S(1)}, f32[1024,128]{1,0:T(8,128)S(1)}, u32[]{:S(2)}, u32[]{:S(2)}) collective-permute-start(f32[1024,128]{1,0:T(8,128)S(1)} %select_select_fusion.2), channel_id=1, source_target_pairs={{64,48},{96,112},{48,32},{80,96},{65,49},{97,113},{49,33},{81,97},... | collective-permute-start | bytes 1572872 | tf_op jit(solution)/shard_map/ppermute | solution.py:228
  56.7 15.1 %collective-permute-start.12 = (f32[1024,128]{1,0:T(8,128)S(1)}, f32[1024,128]{1,0:T(8,128)S(1)}, u32[]{:S(2)}, u32[]{:S(2)}) collective-permute-start(f32[1024,128]{1,0:T(8,128)S(1)} %bitcast.15), channel_id=1, source_target_pairs={{0,128},{128,0},{1,129},{129,1},{2,130},{130,2},{3,131},{131,3},{4... | collective-permute-start | bytes 1572872 | tf_op jit(solution)/shard_map/ppermute | solution.py:225

commit v3 on v2

--- a/solution.py
+++ b/solution.py
@@ -136,7 +136,7 @@
     y = ids[2] // 4
     for j in range(4):
         at = pl.multiple_of(lax.rem(y - j + 4, 4) * 64, 64)
-        out[pl.ds(at, 64), :] = tile_from(pieces[j].at[k])
+        out[pl.ds(at, 64), :] = tile_from(pieces.at[j, k])
 
 
 def first_tile(ref):
@@ -152,13 +152,16 @@
             out_ref[pl.ds(q, NB, stride=2), :] = inv[:, q * LANES : (q + 1) * LANES]
 
 
-def second_kernel(ids, a, b, c, d, inv0_ref, up_ref, inv_ref, work, prev):
-    pieces = (a, b, c, d)
-    tiles_from(ids, pieces, 0, inv0_ref)
-    tiles_from(ids, pieces, 1, work)
-    up = dot(inv0_ref[...], work[...], 1, 1)
+def second_kernel(ids, own, other, inv0_ref, up_ref, inv_ref, lower, work, prev):
+    def place(upper, under):
+        tiles_from(ids, upper, 0, inv0_ref)
+        tiles_from(ids, under, 0, lower)
+        tiles_from(ids, under, 1, work)
+
+    pl.when(ids[0] == 0)(lambda: place(own, other))
+    pl.when(ids[0] != 0)(lambda: place(other, own))
+    up = dot(inv0_ref[...], lower[...], 1, 1)
     up_ref[...] = up
-    tiles_from(ids, pieces, 2, work)
     work[...] = work[...] - dot(up, up, 0, 0)
     inv_ref[...] = factor(work, prev)
 
@@ -248,31 +251,33 @@
     first_rows = pl.BlockSpec((1024, LANES), lambda i, ids: (0, 0))
     (inv0,) = call(first_kernel, ids, (flat,), [first_rows], [(512, LANES)], scratch, 10**10)
 
-    block = lax.dynamic_slice_in_dim(flat, depth * 2048, 2048, 0)
-    strip = block.reshape(512, 4, LANES)[:, :2].reshape(1024, LANES)
+    strip = lax.dynamic_slice(gram_slab, (2 * depth, 0, 0, 0, 0, 0), (2, 1, NB, 1, 1, NB)).reshape(1024, LANES)
     y = depth // 4
     tile = lax.dynamic_slice_in_dim(flat, y * 256, 256, 0).reshape(64, 4, LANES)[:, :2]
     inv0 = lax.dynamic_slice_in_dim(inv0, y * 128, 128, 0)
     tile = jnp.where((row == 0) & (col == 0), inv0, tile.reshape(128, LANES))
+    strip, tile = lax.optimization_barrier((strip, tile))
+    x_b = send(strip, [(0, 1), (1, 0)])
     x_a = send(strip, [(0, 5), (1, 4)])
-    x_b = send(strip, [(0, 1), (1, 0)])
     tile = held_of(tile, *far(tile))
-    tile, x_a, x_b = lax.optimization_barrier((tile, x_a, x_b))
     mine = jnp.stack(both_of(tile, *near(tile)))
+    mine, x_a, x_b = lax.optimization_barrier((mine, x_a, x_b))
     x_c = send(choose(col, [(x_a, ()), (x_b, (1,))]), [(1, 2), (5, 4), (4, 3)])
     x_d = send(choose(col, [(x_a, ()), (x_b, (0,))]), [(5, 6), (4, 5), (0, 7)])
-    other = swap(mine)
-    upper, lower = jnp.where(row == 0, mine, other), jnp.where(row == 0, other, mine)
-    tiles = jnp.stack([upper[0], lower[0], lower[1]])
-    pieces = [tiles] + [
-        lax.ppermute(tiles, "depth", [(d, (d + 4 * j) % 16) for d in range(16)]) for j in (1, 2, 3)
-    ]
-
-    x_c, x_d, own_rows, *pieces = lax.optimization_barrier((x_c, x_d, flat[: NB * 4], *pieces))
+    own = jnp.stack(
+        [mine] + [lax.ppermute(mine, "depth", [(d, (d + 4 * j) % 16) for d in range(16)]) for j in (1, 2, 3)]
+    )
+    x_c, x_d, own = lax.optimization_barrier((x_c, x_d, own))
+    other = swap(own)
+
+    late_slab, own = lax.optimization_barrier((flat, own))
+    block = lax.dynamic_slice_in_dim(late_slab, depth * 2048, 2048, 0)
+    own_rows = late_slab[: NB * 4]
+    own, other = lax.optimization_barrier((own, other))
     other_rows = swap(own_rows)
     x_e = send(choose(col, [(x_c, ()), (x_d, (5, 6))]), [(4, 3), (6, 7), (3, 2), (5, 6)])
     inv0, up, inv1 = call(
-        second_kernel, ids, pieces, [whole(tiles.shape)] * 4, [(NB, NB)] * 3, scratch, 10**10
+        second_kernel, ids, (own, other), [whole(own.shape)] * 2, [(NB, NB)] * 3, [(NB, NB)] + scratch, 10**10
     )
     x_e, inv1 = lax.optimization_barrier((x_e, inv1))
     x0 = choose(col, [(x_e, ()), (strip, (0,)), (x_b, (1,)), (x_c, (2, 4)), (x_a, (5,)), (x_d, (6,))])

time: 79.2 us -> 73.5 us (0.928)
  the two profiles are of different devices: /device:TPU:100 before, /device:TPU:189 now
where the time goes in v3:
time: 73.5 us; the launch traced here: 73 us
  starting transfers between devices  23 us (31%)
  waiting for transfers between devices  21.7 us (30%)
  Pallas kernels  20.6 us (28%)
  local copies, waits for them, and re-layouts  4.71 us (6%)
  other arithmetic  2.69 us (4%)
    pallas_call x3, Pallas kernels, call(): pl.pallas_call(kernel, out_shape=[jax.ShapeDtypeStruct(s, jnp.float32) fo...  20.6 us
    ppermute x9, starting transfers between devices, send(): return lax.ppermute(x, 'col', pairs)  17.9 us
    ppermute x9, waiting for transfers between devices, send(): return lax.ppermute(x, 'col', pairs)  15.2 us
    ppermute x3, waiting for transfers between devices, shards(): lax.ppermute(mine, 'depth', [(d, (d + 4 * j) % 16) for d in range(16)])  6.46 us
    ppermute x2, starting transfers between devices, swap(): return lax.ppermute(x, 'row', [(0, 1), (1, 0)])  2.83 us
    select_n x4, other arithmetic, choose(): out = jnp.where(col == c, value, out)  2.51 us
    ppermute x3, starting transfers between devices, shards(): lax.ppermute(mine, 'depth', [(d, (d + 4 * j) % 16) for d in range(16)])  2.32 us
  transfers between devices with their start and end apart: 14, of which 7 were waited for; matrix products, arithmetic and copies ran while one was open for 7% of the time, Pallas kernels for 16%

profile of v3, /device:TPU:189, one launch (start us, length us, event | category | flops | bytes accessed | tf_op | source)
XLA Modules:
  0.0 73.0 jit_solution(3858394633538259781)
XLA Ops:
  0.0 0.9 %constant_dynamic-slice_fusion.1 = f32[256,128]{1,0:T(8,128)S(1)} fusion(f32[32768,128]{1,0:T(8,128)} %bitcast.20, s32[]{:T(128)S(6)} %select_n.186), kind=kLoop, calls=%fused_computation.19 | loop fusion | bytes 262148 | tf_op jit(solution)/shard_map/dynamic_slice | solution.py:256
  1.0 0.1 pad_add_fusion.ids
  1.0 1.6 %shard_map.17 = f32[512,128]{1,0:T(8,128)S(1)} custom-call(s32[3]{0:T(128)S(1)} %pad_add_fusion.ids, f32[32768,128]{1,0:T(8,128)} %bitcast.21), custom_call_target="tpu_custom_call" | custom-call | flops 10000000000 | bytes 1048576 | tf_op jit(solution)/shard_map/pallas_call | solution.py:197
  2.6 1.4 %constant_dynamic-slice_fusion.2 = f32[2,1,256,1,1,256]{5,4,3,2,1,0:T(1,128)S(1)} fusion(f32[32,1,256,2,1,256]{5,4,3,2,1,0:T(1,128)} %param.1, s32[]{:T(128)S(6)} %select_n.182), kind=kLoop, calls=%fused_computation.20 | loop fusion | bytes 1048580 | tf_op jit(solution)/shard_map/dynamic_slice | solution.py:254
  4.1 1.3 %collective-permute-start = (f32[128,128]{1,0:T(8,128)S(1)}, f32[128,128]{1,0:T(8,128)S(1)}, u32[]{:S(2)}, u32[]{:S(2)}) collective-permute-start(f32[128,128]{1,0:T(8,128)S(1)} %dynamic-slice_select_fusion), channel_id=1, source_target_pairs={{0,80},{16,96},{1,81},{17,97},{2,82},{18,98},{3,83},{19,99},{4,84}... | collective-permute-start | bytes 196616 | tf_op jit(solution)/shard_map/ppermute | solution.py:231
  5.4 0.7 collective-permute-start.1
  6.0 1.3 %collective-permute-start.4 = (f32[1024,128]{1,0:T(8,128)S(1)}, f32[1024,128]{1,0:T(8,128)S(1)}, u32[]{:S(2)}, u32[]{:S(2)}) collective-permute-start(f32[1024,128]{1,0:T(8,128)S(1)} %bitcast.16), channel_id=1, source_target_pairs={{0,80},{16,64},{1,81},{17,65},{2,82},{18,66},{3,83},{19,67},{4,84}... | collective-permute-start | bytes 1572872 | tf_op jit(solution)/shard_map/ppermute | solution.py:231
  7.3 0.7 collective-permute-start.5
  8.0 4.7 %collective-permute-done = f32[128,128]{1,0:T(8,128)S(1)} collective-permute-done((f32[128,128]{1,0:T(8,128)S(1)}, f32[128,128]{1,0:T(8,128)S(1)}, u32[]{:S(2)}, u32[]{:S(2)}) %collective-permute-start) | collective-permute-done | bytes 65568 | tf_op jit(solution)/shard_map/ppermute | solution.py:231
  12.8 0.0 collective-permute-done.1
  12.8 0.7 collective-permute-start.2
  13.5 2.0 %collective-permute-start.3 = (f32[128,128]{1,0:T(8,128)S(1)}, f32[128,128]{1,0:T(8,128)S(1)}, u32[]{:S(2)}, u32[]{:S(2)}) collective-permute-start(f32[128,128]{1,0:T(8,128)S(1)} %select_select_fusion.7), channel_id=1, source_target_pairs={{0,16},{48,64},{80,96},{16,32},{64,80},{96,112},{1,17},{49,65},{81... | collective-permute-start | bytes 196616 | tf_op jit(solution)/shard_map/ppermute | solution.py:231
  15.5 5.2 %collective-permute-done.3 = f32[128,128]{1,0:T(8,128)S(1)} collective-permute-done((f32[128,128]{1,0:T(8,128)S(1)}, f32[128,128]{1,0:T(8,128)S(1)}, u32[]{:S(2)}, u32[]{:S(2)}) %collective-permute-start.3) | collective-permute-done | bytes 65568 | tf_op jit(solution)/shard_map/ppermute | solution.py:231
  20.8 2.2 %collective-permute-done.4 = f32[1024,128]{1,0:T(8,128)S(1)} collective-permute-done((f32[1024,128]{1,0:T(8,128)S(1)}, f32[1024,128]{1,0:T(8,128)S(1)}, u32[]{:S(2)}, u32[]{:S(2)}) %collective-permute-start.4) | collective-permute-done | bytes 524320 | tf_op jit(solution)/shard_map/ppermute | solution.py:231
  23.0 0.1 broadcast_select_fusion
  23.1 7.3 %collective-permute-start.6 = (f32[1024,128]{1,0:T(8,128)S(1)}, f32[1024,128]{1,0:T(8,128)S(1)}, u32[]{:S(2)}, u32[]{:S(2)}) collective-permute-start(f32[1024,128]{1,0:T(8,128)S(1)} %get-tuple-element.42), channel_id=1, source_target_pairs={{16,32},{80,64},{64,48},{17,33},{81,65},{65,49},{18,34},{82,66},{6... | collective-permute-start | bytes 1572872 | tf_op jit(solution)/shard_map/ppermute | solution.py:231
  30.4 1.9 %collective-permute-start.7 = (f32[1024,128]{1,0:T(8,128)S(1)}, f32[1024,128]{1,0:T(8,128)}, u32[]{:S(2)}, u32[]{:S(2)}) collective-permute-start(f32[1024,128]{1,0:T(8,128)S(1)} %get-tuple-element.41), channel_id=1, source_target_pairs={{80,96},{64,80},{0,112},{81,97},{65,81},{1,113},{82,98},{66,82},{2... | collective-permute-start | bytes 1572872 | tf_op jit(solution)/shard_map/ppermute | solution.py:231
  32.3 0.1 collective-permute-start.8
  32.4 2.2 %collective-permute-start.9 = (f32[2,128,128]{2,1,0:T(8,128)S(1)}, f32[2,128,128]{2,1,0:T(8,128)S(1)}, u32[]{:S(2)}, u32[]{:S(2)}) collective-permute-start(f32[2,128,128]{2,1,0:T(8,128)S(1)} %pad_maximum_fusion.1), channel_id=1, source_target_pairs={{0,8},{1,9},{2,10},{3,11},{4,12},{5,13},{6,14},{7,15},{8,0},{9,1},... | collective-permute-start | bytes 393224 | tf_op jit(solution)/shard_map/ppermute | solution.py:268
  34.7 1.6 %collective-permute-done.8 = f32[2,128,128]{2,1,0:T(8,128)S(1)} collective-permute-done((f32[2,128,128]{2,1,0:T(8,128)S(1)}, f32[2,128,128]{2,1,0:T(8,128)S(1)}, u32[]{:S(2)}, u32[]{:S(2)}) %collective-permute-start.8) | collective-permute-done | bytes 131104 | tf_op jit(solution)/shard_map/ppermute | solution.py:268
  36.2 1.6 %collective-permute-done.9 = f32[2,128,128]{2,1,0:T(8,128)S(1)} collective-permute-done((f32[2,128,128]{2,1,0:T(8,128)S(1)}, f32[2,128,128]{2,1,0:T(8,128)S(1)}, u32[]{:S(2)}, u32[]{:S(2)}) %collective-permute-start.9) | collective-permute-done | bytes 131104 | tf_op jit(solution)/shard_map/ppermute | solution.py:268
  37.8 3.3 %collective-permute-done.10 = f32[2,128,128]{2,1,0:T(8,128)S(1)} collective-permute-done((f32[2,128,128]{2,1,0:T(8,128)S(1)}, f32[2,128,128]{2,1,0:T(8,128)S(1)}, u32[]{:S(2)}, u32[]{:S(2)}) %collective-permute-start.10) | collective-permute-done | bytes 131104 | tf_op jit(solution)/shard_map/ppermute | solution.py:268
  41.2 3.1 %collective-permute-done.7 = f32[1024,128]{1,0:T(8,128)} collective-permute-done((f32[1024,128]{1,0:T(8,128)S(1)}, f32[1024,128]{1,0:T(8,128)}, u32[]{:S(2)}, u32[]{:S(2)}) %collective-permute-start.7) | collective-permute-done | bytes 524320 | tf_op jit(solution)/shard_map/ppermute | solution.py:231
  44.3 2.5 %collective-permute-start.13 = (f32[4,2,128,128]{3,2,1,0:T(8,128)S(1)}, f32[4,2,128,128]{3,2,1,0:T(8,128)S(1)}, u32[]{:S(2)}, u32[]{:S(2)}) collective-permute-start(f32[4,2,128,128]{3,2,1,0:T(8,128)S(1)} %pad_maximum_fusion.own), channel_id=1, source_target_pairs={{0,128},{128,0},{1,129},{129,1},{2,130},{130,2},{3,131},{131,3},{4... | collective-permute-start | bytes 1572872 | tf_op jit(solution)/shard_map/ppermute | solution.py:228
  46.7 1.1 %select_select_fusion.2 = f32[1024,128]{1,0:T(8,128)S(1)} fusion(f32[1024,128]{1,0:T(8,128)} %collective-permute-done.7, f32[1024,128]{1,0:T(8,128)S(1)} %collective-permute-done.6, pred[]{:T(512)S(6)} %eq.23, pred[]{:T(512)S(6)} %eq.20), kind=kLoop, calls=%fused_computation.2 | loop fusion | flops 262144 | bytes 1572866 | tf_op jit(solution)/shard_map/jit(_where)/select_n | solution.py:216
  47.9 1.9 %collective-permute-start.12 = (f32[1024,128]{1,0:T(8,128)S(1)}, f32[1024,128]{1,0:T(8,128)S(1)}, u32[]{:S(2)}, u32[]{:S(2)}) collective-permute-start(f32[1024,128]{1,0:T(8,128)S(1)} %select_select_fusion.2), channel_id=1, source_target_pairs={{64,48},{96,112},{48,32},{80,96},{65,49},{97,113},{49,33},{81,97},... | collective-permute-start | bytes 1572872 | tf_op jit(solution)/shard_map/ppermute | solution.py:231
  49.8 1.1 %slice.7.own_rows = f32[1024,128]{1,0:T(8,128)S(1)} slice(f32[32768,128]{1,0:T(8,128)} %bitcast.22), slice={[0:1024], [0:128]} | slice | bytes 1048576 | tf_op jit(solution)/shard_map/slice | solution.py:275
  50.9 0.4 collective-permute-start.11
  51.3 1.3 %constant_dynamic-slice_fusion.slab = f32[2048,128]{1,0:T(8,128)S(1)} fusion(f32[32768,128]{1,0:T(8,128)} %bitcast.23, s32[]{:T(128)S(6)} %select_n.211), kind=kLoop, calls=%fused_computation.18 | loop fusion | bytes 2097156 | tf_op jit(solution)/shard_map/dynamic_slice | solution.py:274
  52.6 12.0 %shard_map.18 = (f32[256,256]{1,0:T(8,128)S(1)}, f32[256,256]{1,0:T(8,128)S(1)}, f32[256,256]{1,0:T(8,128)S(1)}) custom-call(s32[3]{0:T(128)S(1)} %pad_add_fusion.ids, f32[4,2,128,128]{3,2,1,0:T(8,128)S(1)} %pad_maximum_fusion.own, f32[4,2,128,128]{3,2,1,0:T(8,128)S(1)} %collective-permute-done.13.other), custom_call_target="tpu_custom_call" | custom-call | flops 10000000000 | bytes 1048576 | tf_op jit(solution)/shard_map/pallas_call | solution.py:197
  64.6 1.3 %select_select_fusion = (f32[1024,128]{1,0:T(8,128)S(1)}, f32[1024,128]{1,0:T(8,128)S(1)}) fusion(f32[1024,128]{1,0:T(8,128)} %collective-permute-done.7, f32[1024,128]{1,0:T(8,128)S(1)} %collective-permute-done.4, f32[1024,128]{1,0:T(8,128)S(1)} %collective-permute-done.6, f32[1024,128]{1,0:T(8,128)S(1)} %bitcast.18, ...), kind=kLoop, calls=%fused_computation | loop fusion | flops 1572864 | bytes 4194312 | tf_op jit(solution)/shard_map/jit(_where)/select_n | solution.py:216
  65.9 7.0 %shard_map.19 = f32[2048,128]{1,0:T(8,128)} custom-call(s32[3]{0:T(128)S(1)} %pad_add_fusion.ids, f32[2048,128]{1,0:T(8,128)S(1)} %constant_dynamic-slice_fusion.slab, f32[1024,128]{1,0:T(8,128)S(1)} %slice.7.own_rows, f32[1024,128]{1,0:T(8,128)S(1)} %collective-permute-done.11.other_rows, f32[1024,128]{1,0:T(8,128)S(1)} %get-tuple-element.40.x0, ...), custom_call_target="tpu_custom_call" | custom-call | flops 1000000000 | bytes 1048576 | tf_op jit(solution)/shard_map/pallas_call | solution.py:197
  (13 shorter events, 0.2 us)
Async XLA Ops:
  4.1 8.7 %collective-permute-start = (f32[128,128]{1,0:T(8,128)S(1)}, f32[128,128]{1,0:T(8,128)S(1)}, u32[]{:S(2)}, u32[]{:S(2)}) collective-permute-start(f32[128,128]{1,0:T(8,128)S(1)} %dynamic-slice_select_fusion), channel_id=1, source_target_pairs={{0,80},{16,96},{1,81},{17,97},{2,82},{18,98},{3,83},{19,99},{4,84}... | collective-permute-start | bytes 196616 | tf_op jit(solution)/shard_map/ppermute | solution.py:231
  5.4 7.4 %collective-permute-start.1 = (f32[128,128]{1,0:T(8,128)S(1)}, f32[128,128]{1,0:T(8,128)S(1)}, u32[]{:S(2)}, u32[]{:S(2)}) collective-permute-start(f32[128,128]{1,0:T(8,128)S(1)} %dynamic-slice_select_fusion), channel_id=1, source_target_pairs={{0,48},{16,64},{1,49},{17,65},{2,50},{18,66},{3,51},{19,67},{4,52}... | collective-permute-start | bytes 196616 | tf_op jit(solution)/shard_map/ppermute | solution.py:231
  6.0 16.9 %collective-permute-start.4 = (f32[1024,128]{1,0:T(8,128)S(1)}, f32[1024,128]{1,0:T(8,128)S(1)}, u32[]{:S(2)}, u32[]{:S(2)}) collective-permute-start(f32[1024,128]{1,0:T(8,128)S(1)} %bitcast.16), channel_id=1, source_target_pairs={{0,80},{16,64},{1,81},{17,65},{2,82},{18,66},{3,83},{19,67},{4,84}... | collective-permute-start | bytes 1572872 | tf_op jit(solution)/shard_map/ppermute | solution.py:231
  7.3 15.7 %collective-permute-start.5 = (f32[1024,128]{1,0:T(8,128)S(1)}, f32[1024,128]{1,0:T(8,128)S(1)}, u32[]{:S(2)}, u32[]{:S(2)}) collective-permute-start(f32[1024,128]{1,0:T(8,128)S(1)} %bitcast.17), channel_id=1, source_target_pairs={{0,16},{16,0},{1,17},{17,1},{2,18},{18,2},{3,19},{19,3},{4,20},{20... | collective-permute-start | bytes 1572872 | tf_op jit(solution)/shard_map/ppermute | solution.py:231
  12.8 2.7 %collective-permute-start.2 = (f32[128,128]{1,0:T(8,128)S(1)}, f32[128,128]{1,0:T(8,128)S(1)}, u32[]{:S(2)}, u32[]{:S(2)}) collective-permute-start(f32[128,128]{1,0:T(8,128)S(1)} %select_select_fusion.7), channel_id=1, source_target_pairs={{0,112},{48,32},{16,0},{64,48},{1,113},{49,33},{17,1},{65,49},{2,1... | collective-permute-start | bytes 196616 | tf_op jit(solution)/shard_map/ppermute | solution.py:231
  13.5 7.3 %collective-permute-start.3 = (f32[128,128]{1,0:T(8,128)S(1)}, f32[128,128]{1,0:T(8,128)S(1)}, u32[]{:S(2)}, u32[]{:S(2)}) collective-permute-start(f32[128,128]{1,0:T(8,128)S(1)} %select_select_fusion.7), channel_id=1, source_target_pairs={{0,16},{48,64},{80,96},{16,32},{64,80},{96,112},{1,17},{49,65},{81... | collective-permute-start | bytes 196616 | tf_op jit(solution)/shard_map/ppermute | solution.py:231
  23.1 18.1 %collective-permute-start.6 = (f32[1024,128]{1,0:T(8,128)S(1)}, f32[1024,128]{1,0:T(8,128)S(1)}, u32[]{:S(2)}, u32[]{:S(2)}) collective-permute-start(f32[1024,128]{1,0:T(8,128)S(1)} %get-tuple-element.42), channel_id=1, source_target_pairs={{16,32},{80,64},{64,48},{17,33},{81,65},{65,49},{18,34},{82,66},{6... | collective-permute-start | bytes 1572872 | tf_op jit(solution)/shard_map/ppermute | solution.py:231
  30.4 13.9 %collective-permute-start.7 = (f32[1024,128]{1,0:T(8,128)S(1)}, f32[1024,128]{1,0:T(8,128)}, u32[]{:S(2)}, u32[]{:S(2)}) collective-permute-start(f32[1024,128]{1,0:T(8,128)S(1)} %get-tuple-element.41), channel_id=1, source_target_pairs={{80,96},{64,80},{0,112},{81,97},{65,81},{1,113},{82,98},{66,82},{2... | collective-permute-start | bytes 1572872 | tf_op jit(solution)/shard_map/ppermute | solution.py:231
  32.3 3.9 %collective-permute-start.8 = (f32[2,128,128]{2,1,0:T(8,128)S(1)}, f32[2,128,128]{2,1,0:T(8,128)S(1)}, u32[]{:S(2)}, u32[]{:S(2)}) collective-permute-start(f32[2,128,128]{2,1,0:T(8,128)S(1)} %pad_maximum_fusion.1), channel_id=1, source_target_pairs={{0,4},{1,5},{2,6},{3,7},{4,8},{5,9},{6,10},{7,11},{8,12},{9,13},{1... | collective-permute-start | bytes 393224 | tf_op jit(solution)/shard_map/ppermute | solution.py:268
  32.4 5.4 %collective-permute-start.9 = (f32[2,128,128]{2,1,0:T(8,128)S(1)}, f32[2,128,128]{2,1,0:T(8,128)S(1)}, u32[]{:S(2)}, u32[]{:S(2)}) collective-permute-start(f32[2,128,128]{2,1,0:T(8,128)S(1)} %pad_maximum_fusion.1), channel_id=1, source_target_pairs={{0,8},{1,9},{2,10},{3,11},{4,12},{5,13},{6,14},{7,15},{8,0},{9,1},... | collective-permute-start | bytes 393224 | tf_op jit(solution)/shard_map/ppermute | solution.py:268
  34.7 6.5 %collective-permute-start.10 = (f32[2,128,128]{2,1,0:T(8,128)S(1)}, f32[2,128,128]{2,1,0:T(8,128)S(1)}, u32[]{:S(2)}, u32[]{:S(2)}) collective-permute-start(f32[2,128,128]{2,1,0:T(8,128)S(1)} %pad_maximum_fusion.1), channel_id=1, source_target_pairs={{0,12},{1,13},{2,14},{3,15},{4,0},{5,1},{6,2},{7,3},{8,4},{9,5},{1... | collective-permute-start | bytes 393224 | tf_op jit(solution)/shard_map/ppermute | solution.py:268
  44.3 8.3 %collective-permute-start.13 = (f32[4,2,128,128]{3,2,1,0:T(8,128)S(1)}, f32[4,2,128,128]{3,2,1,0:T(8,128)S(1)}, u32[]{:S(2)}, u32[]{:S(2)}) collective-permute-start(f32[4,2,128,128]{3,2,1,0:T(8,128)S(1)} %pad_maximum_fusion.own), channel_id=1, source_target_pairs={{0,128},{128,0},{1,129},{129,1},{2,130},{130,2},{3,131},{131,3},{4... | collective-permute-start | bytes 1572872 | tf_op jit(solution)/shard_map/ppermute | solution.py:228
  47.9 16.7 %collective-permute-start.12 = (f32[1024,128]{1,0:T(8,128)S(1)}, f32[1024,128]{1,0:T(8,128)S(1)}, u32[]{:S(2)}, u32[]{:S(2)}) collective-permute-start(f32[1024,128]{1,0:T(8,128)S(1)} %select_select_fusion.2), channel_id=1, source_target_pairs={{64,48},{96,112},{48,32},{80,96},{65,49},{97,113},{49,33},{81,97},... | collective-permute-start | bytes 1572872 | tf_op jit(solution)/shard_map/ppermute | solution.py:231
  50.9 15.0 %collective-permute-start.11 = (f32[1024,128]{1,0:T(8,128)S(1)}, f32[1024,128]{1,0:T(8,128)S(1)}, u32[]{:S(2)}, u32[]{:S(2)}) collective-permute-start(f32[1024,128]{1,0:T(8,128)S(1)} %slice.7.own_rows), channel_id=1, source_target_pairs={{0,128},{128,0},{1,129},{129,1},{2,130},{130,2},{3,131},{131,3},{4... | collective-permute-start | bytes 1572872 | tf_op jit(solution)/shard_map/ppermute | solution.py:228

commit v4 on v3

--- a/solution.py
+++ b/solution.py
@@ -6,7 +6,7 @@
 from jax.sharding import PartitionSpec as P
 
 NB = 256
-STEP = 32
+STEP = 64
 SUB = 8
 LANES = 128
 highest = lax.Precision.HIGHEST
@@ -143,13 +143,22 @@
     return jnp.concatenate([ref[pl.ds(q, NB, stride=4), :] for q in range(2)], axis=1)
 
 
-def first_kernel(ids, rows, out_ref, work, prev):
+def first_kernel(ids, flat, inv_ref, rows_ref, slab_ref, work, prev, sems):
+    rows = pltpu.make_async_copy(flat.at[pl.ds(0, 4 * NB), :], rows_ref, sems.at[0])
+    start = pl.multiple_of(ids[2] * 8 * NB, 8 * NB)
+    slab = pltpu.make_async_copy(flat.at[pl.ds(start, 8 * NB), :], slab_ref, sems.at[1])
+    rows.start()
+    slab.start()
+    rows.wait()
+
     @pl.when((ids[0] == 0) & (ids[1] == 0))
     def _():
-        work[...] = first_tile(rows)
+        work[...] = first_tile(rows_ref)
         inv = factor(work, prev)
         for q in range(2):
-            out_ref[pl.ds(q, NB, stride=2), :] = inv[:, q * LANES : (q + 1) * LANES]
+            inv_ref[pl.ds(q, NB, stride=2), :] = inv[:, q * LANES : (q + 1) * LANES]
+
+    slab.wait()
 
 
 def second_kernel(ids, own, other, inv0_ref, up_ref, inv_ref, lower, work, prev):
@@ -193,7 +202,7 @@
     return pl.BlockSpec(shape, lambda i, ids: (0,) * len(shape))
 
 
-def call(kernel, ids, args, specs, outs, scratch, flops):
+def call(kernel, ids, args, specs, outs, scratch, flops, vmem):
     return pl.pallas_call(
         kernel,
         out_shape=[jax.ShapeDtypeStruct(s, jnp.float32) for s in outs],
@@ -202,9 +211,9 @@
             grid=(1,),
             in_specs=specs,
             out_specs=[whole(s) for s in outs],
-            scratch_shapes=[pltpu.VMEM(s, jnp.float32) for s in scratch],
+            scratch_shapes=scratch,
         ),
-        compiler_params=pltpu.CompilerParams(vmem_limit_bytes=40 * 1024 * 1024),
+        compiler_params=pltpu.CompilerParams(vmem_limit_bytes=vmem << 20),
         cost_estimate=pl.CostEstimate(flops=flops, bytes_accessed=1 << 20, transcendentals=0),
     )(ids, *args)
 
@@ -247,21 +256,29 @@
         )
 
     square = whole((NB, NB))
-    scratch = [(NB, NB), (STEP, NB)]
-    first_rows = pl.BlockSpec((1024, LANES), lambda i, ids: (0, 0))
-    (inv0,) = call(first_kernel, ids, (flat,), [first_rows], [(512, LANES)], scratch, 10**10)
-
-    strip = lax.dynamic_slice(gram_slab, (2 * depth, 0, 0, 0, 0, 0), (2, 1, NB, 1, 1, NB)).reshape(1024, LANES)
+    scratch = [pltpu.VMEM((NB, NB), jnp.float32), pltpu.VMEM((STEP, NB), jnp.float32)]
+    inv0, own_rows, block = call(
+        first_kernel,
+        ids,
+        (flat,),
+        [pl.BlockSpec(memory_space=pl.ANY)],
+        [(512, LANES), (1024, LANES), (2048, LANES)],
+        scratch + [pltpu.SemaphoreType.DMA((2,))],
+        10**10,
+        40,
+    )
+
+    strip = block.reshape(512, 4, LANES)[:, :2].reshape(1024, LANES)
     y = depth // 4
-    tile = lax.dynamic_slice_in_dim(flat, y * 256, 256, 0).reshape(64, 4, LANES)[:, :2]
+    tile = lax.dynamic_slice_in_dim(own_rows, y * 256, 256, 0).reshape(64, 4, LANES)[:, :2]
     inv0 = lax.dynamic_slice_in_dim(inv0, y * 128, 128, 0)
     tile = jnp.where((row == 0) & (col == 0), inv0, tile.reshape(128, LANES))
     strip, tile = lax.optimization_barrier((strip, tile))
+    x_a = send(strip, [(0, 5), (1, 4)])
     x_b = send(strip, [(0, 1), (1, 0)])
-    x_a = send(strip, [(0, 5), (1, 4)])
     tile = held_of(tile, *far(tile))
     mine = jnp.stack(both_of(tile, *near(tile)))
-    mine, x_a, x_b = lax.optimization_barrier((mine, x_a, x_b))
+    x_b, x_a, mine = lax.optimization_barrier((x_b, x_a, mine))
     x_c = send(choose(col, [(x_a, ()), (x_b, (1,))]), [(1, 2), (5, 4), (4, 3)])
     x_d = send(choose(col, [(x_a, ()), (x_b, (0,))]), [(5, 6), (4, 5), (0, 7)])
     own = jnp.stack(
@@ -270,14 +287,11 @@
     x_c, x_d, own = lax.optimization_barrier((x_c, x_d, own))
     other = swap(own)
 
-    late_slab, own = lax.optimization_barrier((flat, own))
-    block = lax.dynamic_slice_in_dim(late_slab, depth * 2048, 2048, 0)
-    own_rows = late_slab[: NB * 4]
-    own, other = lax.optimization_barrier((own, other))
+    own, other, own_rows = lax.optimization_barrier((own, other, own_rows))
     other_rows = swap(own_rows)
     x_e = send(choose(col, [(x_c, ()), (x_d, (5, 6))]), [(4, 3), (6, 7), (3, 2), (5, 6)])
     inv0, up, inv1 = call(
-        second_kernel, ids, (own, other), [whole(own.shape)] * 2, [(NB, NB)] * 3, [(NB, NB)] + scratch, 10**10
+        second_kernel, ids, (own, other), [whole(own.shape)] * 2, [(NB, NB)] * 3, scratch[:1] + scratch, 10**10, 12
     )
     x_e, inv1 = lax.optimization_barrier((x_e, inv1))
     x0 = choose(col, [(x_e, ()), (strip, (0,)), (x_b, (1,)), (x_c, (2, 4)), (x_a, (5,)), (x_d, (6,))])
@@ -290,6 +304,7 @@
         [(2048, LANES)],
         [],
         10**9,
+        32,
     )
     return out.reshape(2, 1, NB, 2, 1, NB)
 

time: 73.5 us -> 69.2 us (0.941)
  the two profiles are of different devices: /device:TPU:189 before, /device:TPU:100 now
where the time goes in v4:
time: 69.2 us; the launch traced here: 69 us
  waiting for transfers between devices  30.9 us (45%)
  Pallas kernels  20.9 us (30%)
  starting transfers between devices  16.2 us (23%)
    ppermute x9, waiting for transfers between devices, send(): return lax.ppermute(x, 'col', pairs)  23.6 us
    pallas_call x3, Pallas kernels, call(): pl.pallas_call(kernel, out_shape=[jax.ShapeDtypeStruct(s, jnp.float32) fo...  20.9 us
    ppermute x9, starting transfers between devices, send(): return lax.ppermute(x, 'col', pairs)  10.9 us
    ppermute x3, waiting for transfers between devices, shards(): lax.ppermute(mine, 'depth', [(d, (d + 4 * j) % 16) for d in range(16)])  7.32 us
    ppermute x3, starting transfers between devices, shards(): lax.ppermute(mine, 'depth', [(d, (d + 4 * j) % 16) for d in range(16)])  4.7 us
  transfers between devices with their start and end apart: 14, of which 8 were waited for; matrix products, arithmetic and copies ran while one was open for 1% of the time, Pallas kernels for 17%

profile of v4, /device:TPU:100, one launch (start us, length us, event | category | flops | bytes accessed | tf_op | source)
XLA Modules:
  0.0 69.0 jit_solution(844414413839794630)
XLA Ops:
  0.0 0.1 pad_add_fusion.ids
  0.1 1.9 %shard_map.17 = (f32[512,128]{1,0:T(8,128)S(1)}, f32[1024,128]{1,0:T(8,128)S(1)}, f32[2048,128]{1,0:T(8,128)S(1)}) custom-call(s32[3]{0:T(128)S(1)} %pad_add_fusion.ids, f32[32768,128]{1,0:T(8,128)} %bitcast.27), custom_call_target="tpu_custom_call" | custom-call | flops 10000000000 | bytes 1048576 | tf_op jit(solution)/shard_map/pallas_call | solution.py:206
  2.1 0.2 slice.8
  2.3 1.3 %collective-permute-start.3 = (f32[128,128]{1,0:T(8,128)S(1)}, f32[128,128]{1,0:T(8,128)S(1)}, u32[]{:S(2)}, u32[]{:S(2)}) collective-permute-start(f32[128,128]{1,0:T(8,128)S(1)} %dynamic-slice_select_fusion), channel_id=1, source_target_pairs={{0,48},{16,64},{1,49},{17,65},{2,50},{18,66},{3,51},{19,67},{4,52}... | collective-permute-start | bytes 196616 | tf_op jit(solution)/shard_map/ppermute | solution.py:240
  3.6 0.7 collective-permute-start.2
  4.3 0.7 %collective-permute-start.1 = (f32[1024,128]{1,0:T(8,128)S(1)}, f32[1024,128]{1,0:T(8,128)S(1)}, u32[]{:S(2)}, u32[]{:S(2)}) collective-permute-start(f32[1024,128]{1,0:T(8,128)S(1)} %bitcast.18), channel_id=1, source_target_pairs={{0,80},{16,64},{1,81},{17,65},{2,82},{18,66},{3,83},{19,67},{4,84}... | collective-permute-start | bytes 1572872 | tf_op jit(solution)/shard_map/ppermute | solution.py:240
  5.0 0.7 %collective-permute-start = (f32[1024,128]{1,0:T(8,128)S(1)}, f32[1024,128]{1,0:T(8,128)S(1)}, u32[]{:S(2)}, u32[]{:S(2)}) collective-permute-start(f32[1024,128]{1,0:T(8,128)S(1)} %bitcast.19), channel_id=1, source_target_pairs={{0,16},{16,0},{1,17},{17,1},{2,18},{18,2},{3,19},{19,3},{4,20},{20... | collective-permute-start | bytes 1572872 | tf_op jit(solution)/shard_map/ppermute | solution.py:240
  5.7 9.1 %collective-permute-done.3 = f32[128,128]{1,0:T(8,128)S(1)} collective-permute-done((f32[128,128]{1,0:T(8,128)S(1)}, f32[128,128]{1,0:T(8,128)S(1)}, u32[]{:S(2)}, u32[]{:S(2)}) %collective-permute-start.3) | collective-permute-done | bytes 65568 | tf_op jit(solution)/shard_map/ppermute | solution.py:240
  14.8 1.8 %collective-permute-start.5 = (f32[128,128]{1,0:T(8,128)S(1)}, f32[128,128]{1,0:T(8,128)S(1)}, u32[]{:S(2)}, u32[]{:S(2)}) collective-permute-start(f32[128,128]{1,0:T(8,128)S(1)} %select_select_fusion.7), channel_id=1, source_target_pairs={{0,16},{48,64},{80,96},{16,32},{64,80},{96,112},{1,17},{49,65},{81... | collective-permute-start | bytes 196616 | tf_op jit(solution)/shard_map/ppermute | solution.py:240
  16.5 1.9 %collective-permute-start.4 = (f32[128,128]{1,0:T(8,128)S(1)}, f32[128,128]{1,0:T(8,128)S(1)}, u32[]{:S(2)}, u32[]{:S(2)}) collective-permute-start(f32[128,128]{1,0:T(8,128)S(1)} %select_select_fusion.7), channel_id=1, source_target_pairs={{0,112},{48,32},{16,0},{64,48},{1,113},{49,33},{17,1},{65,49},{2,1... | collective-permute-start | bytes 196616 | tf_op jit(solution)/shard_map/ppermute | solution.py:240
  18.5 6.6 %collective-permute-done.5 = f32[128,128]{1,0:T(8,128)S(1)} collective-permute-done((f32[128,128]{1,0:T(8,128)S(1)}, f32[128,128]{1,0:T(8,128)S(1)}, u32[]{:S(2)}, u32[]{:S(2)}) %collective-permute-start.5) | collective-permute-done | bytes 65568 | tf_op jit(solution)/shard_map/ppermute | solution.py:240
  25.1 0.3 collective-permute-done.4
  25.5 0.0 collective-permute-done.1
  25.5 0.1 broadcast_select_fusion
  25.6 0.7 %collective-permute-start.7 = (f32[1024,128]{1,0:T(8,128)S(1)}, f32[1024,128]{1,0:T(8,128)S(1)}, u32[]{:S(2)}, u32[]{:S(2)}) collective-permute-start(f32[1024,128]{1,0:T(8,128)S(1)} %get-tuple-element.45), channel_id=1, source_target_pairs={{80,96},{64,80},{0,112},{81,97},{65,81},{1,113},{82,98},{66,82},{2... | collective-permute-start | bytes 1572872 | tf_op jit(solution)/shard_map/ppermute | solution.py:240
  26.3 1.3 %collective-permute-start.6 = (f32[1024,128]{1,0:T(8,128)S(1)}, f32[1024,128]{1,0:T(8,128)S(1)}, u32[]{:S(2)}, u32[]{:S(2)}) collective-permute-start(f32[1024,128]{1,0:T(8,128)S(1)} %get-tuple-element.46), channel_id=1, source_target_pairs={{16,32},{80,64},{64,48},{17,33},{81,65},{65,49},{18,34},{82,66},{6... | collective-permute-start | bytes 1572872 | tf_op jit(solution)/shard_map/ppermute | solution.py:240
  27.6 3.1 %collective-permute-start.10 = (f32[2,128,128]{2,1,0:T(8,128)S(1)}, f32[2,128,128]{2,1,0:T(8,128)S(1)}, u32[]{:S(2)}, u32[]{:S(2)}) collective-permute-start(f32[2,128,128]{2,1,0:T(8,128)S(1)} %pad_maximum_fusion.1), channel_id=1, source_target_pairs={{0,12},{1,13},{2,14},{3,15},{4,0},{5,1},{6,2},{7,3},{8,4},{9,5},{1... | collective-permute-start | bytes 393224 | tf_op jit(solution)/shard_map/ppermute | solution.py:285
  30.7 0.6 collective-permute-start.9
  31.3 1.0 %collective-permute-start.8 = (f32[2,128,128]{2,1,0:T(8,128)S(1)}, f32[2,128,128]{2,1,0:T(8,128)S(1)}, u32[]{:S(2)}, u32[]{:S(2)}) collective-permute-start(f32[2,128,128]{2,1,0:T(8,128)S(1)} %pad_maximum_fusion.1), channel_id=1, source_target_pairs={{0,4},{1,5},{2,6},{3,7},{4,8},{5,9},{6,10},{7,11},{8,12},{9,13},{1... | collective-permute-start | bytes 393224 | tf_op jit(solution)/shard_map/ppermute | solution.py:285
  32.3 3.6 %collective-permute-done.10 = f32[2,128,128]{2,1,0:T(8,128)S(1)} collective-permute-done((f32[2,128,128]{2,1,0:T(8,128)S(1)}, f32[2,128,128]{2,1,0:T(8,128)S(1)}, u32[]{:S(2)}, u32[]{:S(2)}) %collective-permute-start.10) | collective-permute-done | bytes 131104 | tf_op jit(solution)/shard_map/ppermute | solution.py:285
  35.9 2.3 %collective-permute-done.9 = f32[2,128,128]{2,1,0:T(8,128)S(1)} collective-permute-done((f32[2,128,128]{2,1,0:T(8,128)S(1)}, f32[2,128,128]{2,1,0:T(8,128)S(1)}, u32[]{:S(2)}, u32[]{:S(2)}) %collective-permute-start.9) | collective-permute-done | bytes 131104 | tf_op jit(solution)/shard_map/ppermute | solution.py:285
  38.2 1.4 %collective-permute-done.8 = f32[2,128,128]{2,1,0:T(8,128)S(1)} collective-permute-done((f32[2,128,128]{2,1,0:T(8,128)S(1)}, f32[2,128,128]{2,1,0:T(8,128)S(1)}, u32[]{:S(2)}, u32[]{:S(2)}) %collective-permute-start.8) | collective-permute-done | bytes 131104 | tf_op jit(solution)/shard_map/ppermute | solution.py:285
  39.6 0.0 collective-permute-done.7
  39.6 4.6 %collective-permute-done.6 = f32[1024,128]{1,0:T(8,128)S(1)} collective-permute-done((f32[1024,128]{1,0:T(8,128)S(1)}, f32[1024,128]{1,0:T(8,128)S(1)}, u32[]{:S(2)}, u32[]{:S(2)}) %collective-permute-start.6) | collective-permute-done | bytes 524320 | tf_op jit(solution)/shard_map/ppermute | solution.py:240
  44.2 0.1 select_select_fusion.2
  44.3 1.9 %collective-permute-start.13 = (f32[1024,128]{1,0:T(8,128)S(1)}, f32[1024,128]{1,0:T(8,128)S(1)}, u32[]{:S(2)}, u32[]{:S(2)}) collective-permute-start(f32[1024,128]{1,0:T(8,128)S(1)} %select_select_fusion.2), channel_id=1, source_target_pairs={{64,48},{96,112},{48,32},{80,96},{65,49},{97,113},{49,33},{81,97},... | collective-permute-start | bytes 1572872 | tf_op jit(solution)/shard_map/ppermute | solution.py:240
  46.2 0.0 collective-permute-done.11.other
  46.2 0.6 collective-permute-start.12
  46.8 11.9 %shard_map.18 = (f32[256,256]{1,0:T(8,128)S(1)}, f32[256,256]{1,0:T(8,128)S(1)}, f32[256,256]{1,0:T(8,128)S(1)}) custom-call(s32[3]{0:T(128)S(1)} %pad_add_fusion.ids, f32[4,2,128,128]{3,2,1,0:T(8,128)S(1)} %pad_maximum_fusion.own, f32[4,2,128,128]{3,2,1,0:T(8,128)S(1)} %collective-permute-done.11.other), custom_call_target="tpu_custom_call" | custom-call | flops 10000000000 | bytes 1048576 | tf_op jit(solution)/shard_map/pallas_call | solution.py:206
  58.7 3.0 %collective-permute-done.13 = f32[1024,128]{1,0:T(8,128)S(1)} collective-permute-done((f32[1024,128]{1,0:T(8,128)S(1)}, f32[1024,128]{1,0:T(8,128)S(1)}, u32[]{:S(2)}, u32[]{:S(2)}) %collective-permute-start.13) | collective-permute-done | bytes 524320 | tf_op jit(solution)/shard_map/ppermute | solution.py:240
  61.7 0.2 select_select_fusion
  62.0 7.0 %shard_map.19 = f32[2048,128]{1,0:T(8,128)} custom-call(s32[3]{0:T(128)S(1)} %pad_add_fusion.ids, f32[2048,128]{1,0:T(8,128)S(1)} %get-tuple-element.24.slab, f32[1024,128]{1,0:T(8,128)S(1)} %get-tuple-element.33.own_rows, f32[1024,128]{1,0:T(8,128)S(1)} %collective-permute-done.12.other_rows, f32[1024,128]{1,0:T(8,128)S(1)} %get-tuple-element.44.x0, ...), custom_call_target="tpu_custom_call" | custom-call | flops 1000000000 | bytes 1048576 | tf_op jit(solution)/shard_map/pallas_call | solution.py:206
  (11 shorter events, 0.2 us)
Async XLA Ops:
  2.3 12.4 %collective-permute-start.3 = (f32[128,128]{1,0:T(8,128)S(1)}, f32[128,128]{1,0:T(8,128)S(1)}, u32[]{:S(2)}, u32[]{:S(2)}) collective-permute-start(f32[128,128]{1,0:T(8,128)S(1)} %dynamic-slice_select_fusion), channel_id=1, source_target_pairs={{0,48},{16,64},{1,49},{17,65},{2,50},{18,66},{3,51},{19,67},{4,52}... | collective-permute-start | bytes 196616 | tf_op jit(solution)/shard_map/ppermute | solution.py:240
  3.6 11.1 %collective-permute-start.2 = (f32[128,128]{1,0:T(8,128)S(1)}, f32[128,128]{1,0:T(8,128)S(1)}, u32[]{:S(2)}, u32[]{:S(2)}) collective-permute-start(f32[128,128]{1,0:T(8,128)S(1)} %dynamic-slice_select_fusion), channel_id=1, source_target_pairs={{0,80},{16,96},{1,81},{17,97},{2,82},{18,98},{3,83},{19,99},{4,84}... | collective-permute-start | bytes 196616 | tf_op jit(solution)/shard_map/ppermute | solution.py:240
  4.3 21.2 %collective-permute-start.1 = (f32[1024,128]{1,0:T(8,128)S(1)}, f32[1024,128]{1,0:T(8,128)S(1)}, u32[]{:S(2)}, u32[]{:S(2)}) collective-permute-start(f32[1024,128]{1,0:T(8,128)S(1)} %bitcast.18), channel_id=1, source_target_pairs={{0,80},{16,64},{1,81},{17,65},{2,82},{18,66},{3,83},{19,67},{4,84}... | collective-permute-start | bytes 1572872 | tf_op jit(solution)/shard_map/ppermute | solution.py:240
  5.0 20.5 %collective-permute-start = (f32[1024,128]{1,0:T(8,128)S(1)}, f32[1024,128]{1,0:T(8,128)S(1)}, u32[]{:S(2)}, u32[]{:S(2)}) collective-permute-start(f32[1024,128]{1,0:T(8,128)S(1)} %bitcast.19), channel_id=1, source_target_pairs={{0,16},{16,0},{1,17},{17,1},{2,18},{18,2},{3,19},{19,3},{4,20},{20... | collective-permute-start | bytes 1572872 | tf_op jit(solution)/shard_map/ppermute | solution.py:240
  14.8 10.3 %collective-permute-start.5 = (f32[128,128]{1,0:T(8,128)S(1)}, f32[128,128]{1,0:T(8,128)S(1)}, u32[]{:S(2)}, u32[]{:S(2)}) collective-permute-start(f32[128,128]{1,0:T(8,128)S(1)} %select_select_fusion.7), channel_id=1, source_target_pairs={{0,16},{48,64},{80,96},{16,32},{64,80},{96,112},{1,17},{49,65},{81... | collective-permute-start | bytes 196616 | tf_op jit(solution)/shard_map/ppermute | solution.py:240
  16.5 8.9 %collective-permute-start.4 = (f32[128,128]{1,0:T(8,128)S(1)}, f32[128,128]{1,0:T(8,128)S(1)}, u32[]{:S(2)}, u32[]{:S(2)}) collective-permute-start(f32[128,128]{1,0:T(8,128)S(1)} %select_select_fusion.7), channel_id=1, source_target_pairs={{0,112},{48,32},{16,0},{64,48},{1,113},{49,33},{17,1},{65,49},{2,1... | collective-permute-start | bytes 196616 | tf_op jit(solution)/shard_map/ppermute | solution.py:240
  25.6 14.1 %collective-permute-start.7 = (f32[1024,128]{1,0:T(8,128)S(1)}, f32[1024,128]{1,0:T(8,128)S(1)}, u32[]{:S(2)}, u32[]{:S(2)}) collective-permute-start(f32[1024,128]{1,0:T(8,128)S(1)} %get-tuple-element.45), channel_id=1, source_target_pairs={{80,96},{64,80},{0,112},{81,97},{65,81},{1,113},{82,98},{66,82},{2... | collective-permute-start | bytes 1572872 | tf_op jit(solution)/shard_map/ppermute | solution.py:240
  26.3 17.9 %collective-permute-start.6 = (f32[1024,128]{1,0:T(8,128)S(1)}, f32[1024,128]{1,0:T(8,128)S(1)}, u32[]{:S(2)}, u32[]{:S(2)}) collective-permute-start(f32[1024,128]{1,0:T(8,128)S(1)} %get-tuple-element.46), channel_id=1, source_target_pairs={{16,32},{80,64},{64,48},{17,33},{81,65},{65,49},{18,34},{82,66},{6... | collective-permute-start | bytes 1572872 | tf_op jit(solution)/shard_map/ppermute | solution.py:240
  27.6 8.3 %collective-permute-start.10 = (f32[2,128,128]{2,1,0:T(8,128)S(1)}, f32[2,128,128]{2,1,0:T(8,128)S(1)}, u32[]{:S(2)}, u32[]{:S(2)}) collective-permute-start(f32[2,128,128]{2,1,0:T(8,128)S(1)} %pad_maximum_fusion.1), channel_id=1, source_target_pairs={{0,12},{1,13},{2,14},{3,15},{4,0},{5,1},{6,2},{7,3},{8,4},{9,5},{1... | collective-permute-start | bytes 393224 | tf_op jit(solution)/shard_map/ppermute | solution.py:285
  30.7 7.6 %collective-permute-start.9 = (f32[2,128,128]{2,1,0:T(8,128)S(1)}, f32[2,128,128]{2,1,0:T(8,128)S(1)}, u32[]{:S(2)}, u32[]{:S(2)}) collective-permute-start(f32[2,128,128]{2,1,0:T(8,128)S(1)} %pad_maximum_fusion.1), channel_id=1, source_target_pairs={{0,8},{1,9},{2,10},{3,11},{4,12},{5,13},{6,14},{7,15},{8,0},{9,1},... | collective-permute-start | bytes 393224 | tf_op jit(solution)/shard_map/ppermute | solution.py:285
  31.3 8.3 %collective-permute-start.8 = (f32[2,128,128]{2,1,0:T(8,128)S(1)}, f32[2,128,128]{2,1,0:T(8,128)S(1)}, u32[]{:S(2)}, u32[]{:S(2)}) collective-permute-start(f32[2,128,128]{2,1,0:T(8,128)S(1)} %pad_maximum_fusion.1), channel_id=1, source_target_pairs={{0,4},{1,5},{2,6},{3,7},{4,8},{5,9},{6,10},{7,11},{8,12},{9,13},{1... | collective-permute-start | bytes 393224 | tf_op jit(solution)/shard_map/ppermute | solution.py:285
  44.2 2.0 %collective-permute-start.11 = (f32[4,2,128,128]{3,2,1,0:T(8,128)S(1)}, f32[4,2,128,128]{3,2,1,0:T(8,128)S(1)}, u32[]{:S(2)}, u32[]{:S(2)}) collective-permute-start(f32[4,2,128,128]{3,2,1,0:T(8,128)S(1)} %pad_maximum_fusion.own), channel_id=1, source_target_pairs={{0,128},{128,0},{1,129},{129,1},{2,130},{130,2},{3,131},{131,3},{4... | collective-permute-start | bytes 1572872 | tf_op jit(solution)/shard_map/ppermute | solution.py:237
  44.3 17.4 %collective-permute-start.13 = (f32[1024,128]{1,0:T(8,128)S(1)}, f32[1024,128]{1,0:T(8,128)S(1)}, u32[]{:S(2)}, u32[]{:S(2)}) collective-permute-start(f32[1024,128]{1,0:T(8,128)S(1)} %select_select_fusion.2), channel_id=1, source_target_pairs={{64,48},{96,112},{48,32},{80,96},{65,49},{97,113},{49,33},{81,97},... | collective-permute-start | bytes 1572872 | tf_op jit(solution)/shard_map/ppermute | solution.py:240
  46.2 15.7 %collective-permute-start.12 = (f32[1024,128]{1,0:T(8,128)S(1)}, f32[1024,128]{1,0:T(8,128)S(1)}, u32[]{:S(2)}, u32[]{:S(2)}) collective-permute-start(f32[1024,128]{1,0:T(8,128)S(1)} %get-tuple-element.33.own_rows), channel_id=1, source_target_pairs={{0,128},{128,0},{1,129},{129,1},{2,130},{130,2},{3,131},{131,3},{4... | collective-permute-start | bytes 1572872 | tf_op jit(solution)/shard_map/ppermute | solution.py:237

commit v5 on v4

--- a/solution.py
+++ b/solution.py
@@ -275,27 +275,29 @@
     tile = jnp.where((row == 0) & (col == 0), inv0, tile.reshape(128, LANES))
     strip, tile = lax.optimization_barrier((strip, tile))
     x_a = send(strip, [(0, 5), (1, 4)])
-    x_b = send(strip, [(0, 1), (1, 0)])
     tile = held_of(tile, *far(tile))
     mine = jnp.stack(both_of(tile, *near(tile)))
-    x_b, x_a, mine = lax.optimization_barrier((x_b, x_a, mine))
-    x_c = send(choose(col, [(x_a, ()), (x_b, (1,))]), [(1, 2), (5, 4), (4, 3)])
-    x_d = send(choose(col, [(x_a, ()), (x_b, (0,))]), [(5, 6), (4, 5), (0, 7)])
+    x_a, mine = lax.optimization_barrier((x_a, mine))
+    held = choose(col, [(x_a, ()), (strip, (0, 1))])
+    x_b = send(held, [(0, 1), (5, 4), (4, 3)])
+    x_c = send(held, [(1, 0), (5, 6), (4, 5)])
     own = jnp.stack(
         [mine] + [lax.ppermute(mine, "depth", [(d, (d + 4 * j) % 16) for d in range(16)]) for j in (1, 2, 3)]
     )
-    x_c, x_d, own = lax.optimization_barrier((x_c, x_d, own))
+    x_b, x_c, own = lax.optimization_barrier((x_b, x_c, own))
     other = swap(own)
 
     own, other, own_rows = lax.optimization_barrier((own, other, own_rows))
     other_rows = swap(own_rows)
-    x_e = send(choose(col, [(x_c, ()), (x_d, (5, 6))]), [(4, 3), (6, 7), (3, 2), (5, 6)])
+    held = choose(col, [(x_b, ()), (x_c, (0, 5, 6))])
+    x_d = send(held, [(4, 3), (6, 7), (3, 2), (5, 6)])
+    x_e = send(held, [(1, 2), (0, 7)])
     inv0, up, inv1 = call(
         second_kernel, ids, (own, other), [whole(own.shape)] * 2, [(NB, NB)] * 3, scratch[:1] + scratch, 10**10, 12
     )
-    x_e, inv1 = lax.optimization_barrier((x_e, inv1))
-    x0 = choose(col, [(x_e, ()), (strip, (0,)), (x_b, (1,)), (x_c, (2, 4)), (x_a, (5,)), (x_d, (6,))])
-    x1 = choose(col, [(x_e, ()), (x_b, (0,)), (strip, (1,)), (x_c, (3,)), (x_a, (4,)), (x_d, (5, 7))])
+    x_d, x_e, inv1 = lax.optimization_barrier((x_d, x_e, inv1))
+    x0 = choose(col, [(x_d, ()), (strip, (0,)), (x_b, (1, 4)), (x_e, (2,)), (x_a, (5,)), (x_c, (6,))])
+    x1 = choose(col, [(x_d, ()), (x_c, (0, 5)), (strip, (1,)), (x_b, (3,)), (x_a, (4,)), (x_e, (7,))])
     (out,) = call(
         last_kernel,
         ids,

time: 69.2 us -> 69.9 us (1.010)
  waiting for transfers between devices: 30.9 us -> 31.6 us
where the time goes in v5:
time: 69.9 us; the launch traced here: 69.7 us
  waiting for transfers between devices  31.6 us (45%)
  Pallas kernels  20.9 us (30%)
  starting transfers between devices  16.2 us (23%)
    ppermute x9, waiting for transfers between devices, send(): return lax.ppermute(x, 'col', pairs)  24.3 us
    pallas_call x3, Pallas kernels, call(): pl.pallas_call(kernel, out_shape=[jax.ShapeDtypeStruct(s, jnp.float32) fo...  20.9 us
    ppermute x9, starting transfers between devices, send(): return lax.ppermute(x, 'col', pairs)  10.9 us
    ppermute x3, waiting for transfers between devices, shards(): lax.ppermute(mine, 'depth', [(d, (d + 4 * j) % 16) for d in range(16)])  7.32 us
    ppermute x3, starting transfers between devices, shards(): lax.ppermute(mine, 'depth', [(d, (d + 4 * j) % 16) for d in range(16)])  4.7 us
  transfers between devices with their start and end apart: 14, of which 8 were waited for; matrix products, arithmetic and copies ran while one was open for 1% of the time, Pallas kernels for 17%

profile of v5, /device:TPU:100, one launch (start us, length us, event | category | flops | bytes accessed | tf_op | source)
XLA Modules:
  0.0 69.7 jit_solution(3911017832667997287)
XLA Ops:
  0.0 0.1 pad_add_fusion.ids
  0.1 1.9 %shard_map.17 = (f32[512,128]{1,0:T(8,128)S(1)}, f32[1024,128]{1,0:T(8,128)S(1)}, f32[2048,128]{1,0:T(8,128)S(1)}) custom-call(s32[3]{0:T(128)S(1)} %pad_add_fusion.ids, f32[32768,128]{1,0:T(8,128)} %bitcast.27), custom_call_target="tpu_custom_call" | custom-call | flops 10000000000 | bytes 1048576 | tf_op jit(solution)/shard_map/pallas_call | solution.py:206
  2.1 0.2 slice.8
  2.3 1.3 %collective-permute-start.2 = (f32[128,128]{1,0:T(8,128)S(1)}, f32[128,128]{1,0:T(8,128)S(1)}, u32[]{:S(2)}, u32[]{:S(2)}) collective-permute-start(f32[128,128]{1,0:T(8,128)S(1)} %dynamic-slice_select_fusion), channel_id=1, source_target_pairs={{0,48},{16,64},{1,49},{17,65},{2,50},{18,66},{3,51},{19,67},{4,52}... | collective-permute-start | bytes 196616 | tf_op jit(solution)/shard_map/ppermute | solution.py:240
  3.6 0.7 collective-permute-start.1
  4.3 0.7 collective-permute-start
  5.0 9.8 %collective-permute-done.2 = f32[128,128]{1,0:T(8,128)S(1)} collective-permute-done((f32[128,128]{1,0:T(8,128)S(1)}, f32[128,128]{1,0:T(8,128)S(1)}, u32[]{:S(2)}, u32[]{:S(2)}) %collective-permute-start.2) | collective-permute-done | bytes 65568 | tf_op jit(solution)/shard_map/ppermute | solution.py:240
  14.8 0.0 collective-permute-done.1
  14.8 1.8 %collective-permute-start.4 = (f32[128,128]{1,0:T(8,128)S(1)}, f32[128,128]{1,0:T(8,128)S(1)}, u32[]{:S(2)}, u32[]{:S(2)}) collective-permute-start(f32[128,128]{1,0:T(8,128)S(1)} %select_select_fusion.8), channel_id=1, source_target_pairs={{0,16},{48,64},{80,96},{16,32},{64,80},{96,112},{1,17},{49,65},{81... | collective-permute-start | bytes 196616 | tf_op jit(solution)/shard_map/ppermute | solution.py:240
  16.5 1.9 %collective-permute-start.3 = (f32[128,128]{1,0:T(8,128)S(1)}, f32[128,128]{1,0:T(8,128)S(1)}, u32[]{:S(2)}, u32[]{:S(2)}) collective-permute-start(f32[128,128]{1,0:T(8,128)S(1)} %select_select_fusion.8), channel_id=1, source_target_pairs={{0,112},{48,32},{16,0},{64,48},{1,113},{49,33},{17,1},{65,49},{2,1... | collective-permute-start | bytes 196616 | tf_op jit(solution)/shard_map/ppermute | solution.py:240
  18.5 6.6 %collective-permute-done.4 = f32[128,128]{1,0:T(8,128)S(1)} collective-permute-done((f32[128,128]{1,0:T(8,128)S(1)}, f32[128,128]{1,0:T(8,128)S(1)}, u32[]{:S(2)}, u32[]{:S(2)}) %collective-permute-start.4) | collective-permute-done | bytes 65568 | tf_op jit(solution)/shard_map/ppermute | solution.py:240
  25.1 0.3 collective-permute-done.3
  25.5 0.0 collective-permute-done
  25.5 0.1 select_select_fusion.3
  25.5 0.7 collective-permute-start.6
  26.2 1.3 %collective-permute-start.5 = (f32[1024,128]{1,0:T(8,128)S(1)}, f32[1024,128]{1,0:T(8,128)S(1)}, u32[]{:S(2)}, u32[]{:S(2)}) collective-permute-start(f32[1024,128]{1,0:T(8,128)S(1)} %select_select_fusion.3), channel_id=1, source_target_pairs={{0,16},{80,64},{64,48},{1,17},{81,65},{65,49},{2,18},{82,66},{66,5... | collective-permute-start | bytes 1572872 | tf_op jit(solution)/shard_map/ppermute | solution.py:240
  27.5 3.1 %collective-permute-start.9 = (f32[2,128,128]{2,1,0:T(8,128)S(1)}, f32[2,128,128]{2,1,0:T(8,128)S(1)}, u32[]{:S(2)}, u32[]{:S(2)}) collective-permute-start(f32[2,128,128]{2,1,0:T(8,128)S(1)} %pad_maximum_fusion.1), channel_id=1, source_target_pairs={{0,12},{1,13},{2,14},{3,15},{4,0},{5,1},{6,2},{7,3},{8,4},{9,5},{1... | collective-permute-start | bytes 393224 | tf_op jit(solution)/shard_map/ppermute | solution.py:285
  30.6 0.6 collective-permute-start.8
  31.3 1.0 %collective-permute-start.7 = (f32[2,128,128]{2,1,0:T(8,128)S(1)}, f32[2,128,128]{2,1,0:T(8,128)S(1)}, u32[]{:S(2)}, u32[]{:S(2)}) collective-permute-start(f32[2,128,128]{2,1,0:T(8,128)S(1)} %pad_maximum_fusion.1), channel_id=1, source_target_pairs={{0,4},{1,5},{2,6},{3,7},{4,8},{5,9},{6,10},{7,11},{8,12},{9,13},{1... | collective-permute-start | bytes 393224 | tf_op jit(solution)/shard_map/ppermute | solution.py:285
  32.2 3.6 %collective-permute-done.9 = f32[2,128,128]{2,1,0:T(8,128)S(1)} collective-permute-done((f32[2,128,128]{2,1,0:T(8,128)S(1)}, f32[2,128,128]{2,1,0:T(8,128)S(1)}, u32[]{:S(2)}, u32[]{:S(2)}) %collective-permute-start.9) | collective-permute-done | bytes 131104 | tf_op jit(solution)/shard_map/ppermute | solution.py:285
  35.9 2.3 %collective-permute-done.8 = f32[2,128,128]{2,1,0:T(8,128)S(1)} collective-permute-done((f32[2,128,128]{2,1,0:T(8,128)S(1)}, f32[2,128,128]{2,1,0:T(8,128)S(1)}, u32[]{:S(2)}, u32[]{:S(2)}) %collective-permute-start.8) | collective-permute-done | bytes 131104 | tf_op jit(solution)/shard_map/ppermute | solution.py:285
  38.2 1.4 %collective-permute-done.7 = f32[2,128,128]{2,1,0:T(8,128)S(1)} collective-permute-done((f32[2,128,128]{2,1,0:T(8,128)S(1)}, f32[2,128,128]{2,1,0:T(8,128)S(1)}, u32[]{:S(2)}, u32[]{:S(2)}) %collective-permute-start.7) | collective-permute-done | bytes 131104 | tf_op jit(solution)/shard_map/ppermute | solution.py:285
  39.6 0.0 collective-permute-done.6
  39.6 4.6 %collective-permute-done.5 = f32[1024,128]{1,0:T(8,128)S(1)} collective-permute-done((f32[1024,128]{1,0:T(8,128)S(1)}, f32[1024,128]{1,0:T(8,128)S(1)}, u32[]{:S(2)}, u32[]{:S(2)}) %collective-permute-start.5) | collective-permute-done | bytes 524320 | tf_op jit(solution)/shard_map/ppermute | solution.py:240
  44.2 0.1 select_select_fusion.2
  44.3 0.7 collective-permute-start.13
  45.0 1.9 %collective-permute-start.12 = (f32[1024,128]{1,0:T(8,128)S(1)}, f32[1024,128]{1,0:T(8,128)S(1)}, u32[]{:S(2)}, u32[]{:S(2)}) collective-permute-start(f32[1024,128]{1,0:T(8,128)S(1)} %select_select_fusion.2), channel_id=1, source_target_pairs={{64,48},{96,112},{48,32},{80,96},{65,49},{97,113},{49,33},{81,97},... | collective-permute-start | bytes 1572872 | tf_op jit(solution)/shard_map/ppermute | solution.py:240
  46.9 0.6 collective-permute-start.11
  47.5 11.9 %shard_map.18 = (f32[256,256]{1,0:T(8,128)S(1)}, f32[256,256]{1,0:T(8,128)S(1)}, f32[256,256]{1,0:T(8,128)S(1)}) custom-call(s32[3]{0:T(128)S(1)} %pad_add_fusion.ids, f32[4,2,128,128]{3,2,1,0:T(8,128)S(1)} %pad_maximum_fusion.own, f32[4,2,128,128]{3,2,1,0:T(8,128)S(1)} %collective-permute-done.10.other), custom_call_target="tpu_custom_call" | custom-call | flops 10000000000 | bytes 1048576 | tf_op jit(solution)/shard_map/pallas_call | solution.py:206
  59.4 3.0 %collective-permute-done.12 = f32[1024,128]{1,0:T(8,128)S(1)} collective-permute-done((f32[1024,128]{1,0:T(8,128)S(1)}, f32[1024,128]{1,0:T(8,128)S(1)}, u32[]{:S(2)}, u32[]{:S(2)}) %collective-permute-start.12) | collective-permute-done | bytes 524320 | tf_op jit(solution)/shard_map/ppermute | solution.py:240
  62.4 0.3 fusion.6
  62.7 7.0 %shard_map.19 = f32[2048,128]{1,0:T(8,128)} custom-call(s32[3]{0:T(128)S(1)} %pad_add_fusion.ids, f32[2048,128]{1,0:T(8,128)S(1)} %get-tuple-element.24.slab, f32[1024,128]{1,0:T(8,128)S(1)} %get-tuple-element.32.own_rows, f32[1024,128]{1,0:T(8,128)S(1)} %collective-permute-done.11.other_rows, f32[1024,128]{1,0:T(8,128)S(1)} %get-tuple-element.44.x0, ...), custom_call_target="tpu_custom_call" | custom-call | flops 1000000000 | bytes 1048576 | tf_op jit(solution)/shard_map/pallas_call | solution.py:206
  (11 shorter events, 0.2 us)
Async XLA Ops:
  2.3 12.4 %collective-permute-start.2 = (f32[128,128]{1,0:T(8,128)S(1)}, f32[128,128]{1,0:T(8,128)S(1)}, u32[]{:S(2)}, u32[]{:S(2)}) collective-permute-start(f32[128,128]{1,0:T(8,128)S(1)} %dynamic-slice_select_fusion), channel_id=1, source_target_pairs={{0,48},{16,64},{1,49},{17,65},{2,50},{18,66},{3,51},{19,67},{4,52}... | collective-permute-start | bytes 196616 | tf_op jit(solution)/shard_map/ppermute | solution.py:240
  3.6 11.1 %collective-permute-start.1 = (f32[128,128]{1,0:T(8,128)S(1)}, f32[128,128]{1,0:T(8,128)S(1)}, u32[]{:S(2)}, u32[]{:S(2)}) collective-permute-start(f32[128,128]{1,0:T(8,128)S(1)} %dynamic-slice_select_fusion), channel_id=1, source_target_pairs={{0,80},{16,96},{1,81},{17,97},{2,82},{18,98},{3,83},{19,99},{4,84}... | collective-permute-start | bytes 196616 | tf_op jit(solution)/shard_map/ppermute | solution.py:240
  4.3 21.2 %collective-permute-start = (f32[1024,128]{1,0:T(8,128)S(1)}, f32[1024,128]{1,0:T(8,128)S(1)}, u32[]{:S(2)}, u32[]{:S(2)}) collective-permute-start(f32[1024,128]{1,0:T(8,128)S(1)} %bitcast.18), channel_id=1, source_target_pairs={{0,80},{16,64},{1,81},{17,65},{2,82},{18,66},{3,83},{19,67},{4,84}... | collective-permute-start | bytes 1572872 | tf_op jit(solution)/shard_map/ppermute | solution.py:240
  14.8 10.3 %collective-permute-start.4 = (f32[128,128]{1,0:T(8,128)S(1)}, f32[128,128]{1,0:T(8,128)S(1)}, u32[]{:S(2)}, u32[]{:S(2)}) collective-permute-start(f32[128,128]{1,0:T(8,128)S(1)} %select_select_fusion.8), channel_id=1, source_target_pairs={{0,16},{48,64},{80,96},{16,32},{64,80},{96,112},{1,17},{49,65},{81... | collective-permute-start | bytes 196616 | tf_op jit(solution)/shard_map/ppermute | solution.py:240
  16.5 8.9 %collective-permute-start.3 = (f32[128,128]{1,0:T(8,128)S(1)}, f32[128,128]{1,0:T(8,128)S(1)}, u32[]{:S(2)}, u32[]{:S(2)}) collective-permute-start(f32[128,128]{1,0:T(8,128)S(1)} %select_select_fusion.8), channel_id=1, source_target_pairs={{0,112},{48,32},{16,0},{64,48},{1,113},{49,33},{17,1},{65,49},{2,1... | collective-permute-start | bytes 196616 | tf_op jit(solution)/shard_map/ppermute | solution.py:240
  25.5 14.1 %collective-permute-start.6 = (f32[1024,128]{1,0:T(8,128)S(1)}, f32[1024,128]{1,0:T(8,128)S(1)}, u32[]{:S(2)}, u32[]{:S(2)}) collective-permute-start(f32[1024,128]{1,0:T(8,128)S(1)} %select_select_fusion.3), channel_id=1, source_target_pairs={{16,0},{80,96},{64,80},{17,1},{81,97},{65,81},{18,2},{82,98},{66,8... | collective-permute-start | bytes 1572872 | tf_op jit(solution)/shard_map/ppermute | solution.py:240
  26.2 17.9 %collective-permute-start.5 = (f32[1024,128]{1,0:T(8,128)S(1)}, f32[1024,128]{1,0:T(8,128)S(1)}, u32[]{:S(2)}, u32[]{:S(2)}) collective-permute-start(f32[1024,128]{1,0:T(8,128)S(1)} %select_select_fusion.3), channel_id=1, source_target_pairs={{0,16},{80,64},{64,48},{1,17},{81,65},{65,49},{2,18},{82,66},{66,5... | collective-permute-start | bytes 1572872 | tf_op jit(solution)/shard_map/ppermute | solution.py:240
  27.5 8.3 %collective-permute-start.9 = (f32[2,128,128]{2,1,0:T(8,128)S(1)}, f32[2,128,128]{2,1,0:T(8,128)S(1)}, u32[]{:S(2)}, u32[]{:S(2)}) collective-permute-start(f32[2,128,128]{2,1,0:T(8,128)S(1)} %pad_maximum_fusion.1), channel_id=1, source_target_pairs={{0,12},{1,13},{2,14},{3,15},{4,0},{5,1},{6,2},{7,3},{8,4},{9,5},{1... | collective-permute-start | bytes 393224 | tf_op jit(solution)/shard_map/ppermute | solution.py:285
  30.6 7.6 %collective-permute-start.8 = (f32[2,128,128]{2,1,0:T(8,128)S(1)}, f32[2,128,128]{2,1,0:T(8,128)S(1)}, u32[]{:S(2)}, u32[]{:S(2)}) collective-permute-start(f32[2,128,128]{2,1,0:T(8,128)S(1)} %pad_maximum_fusion.1), channel_id=1, source_target_pairs={{0,8},{1,9},{2,10},{3,11},{4,12},{5,13},{6,14},{7,15},{8,0},{9,1},... | collective-permute-start | bytes 393224 | tf_op jit(solution)/shard_map/ppermute | solution.py:285
  31.3 8.3 %collective-permute-start.7 = (f32[2,128,128]{2,1,0:T(8,128)S(1)}, f32[2,128,128]{2,1,0:T(8,128)S(1)}, u32[]{:S(2)}, u32[]{:S(2)}) collective-permute-start(f32[2,128,128]{2,1,0:T(8,128)S(1)} %pad_maximum_fusion.1), channel_id=1, source_target_pairs={{0,4},{1,5},{2,6},{3,7},{4,8},{5,9},{6,10},{7,11},{8,12},{9,13},{1... | collective-permute-start | bytes 393224 | tf_op jit(solution)/shard_map/ppermute | solution.py:285
  44.2 2.7 %collective-permute-start.10 = (f32[4,2,128,128]{3,2,1,0:T(8,128)S(1)}, f32[4,2,128,128]{3,2,1,0:T(8,128)S(1)}, u32[]{:S(2)}, u32[]{:S(2)}) collective-permute-start(f32[4,2,128,128]{3,2,1,0:T(8,128)S(1)} %pad_maximum_fusion.own), channel_id=1, source_target_pairs={{0,128},{128,0},{1,129},{129,1},{2,130},{130,2},{3,131},{131,3},{4... | collective-permute-start | bytes 1572872 | tf_op jit(solution)/shard_map/ppermute | solution.py:237
  44.3 15.1 %collective-permute-start.13 = (f32[1024,128]{1,0:T(8,128)S(1)}, f32[1024,128]{1,0:T(8,128)S(1)}, u32[]{:S(2)}, u32[]{:S(2)}) collective-permute-start(f32[1024,128]{1,0:T(8,128)S(1)} %select_select_fusion.2), channel_id=1, source_target_pairs={{16,32},{0,112},{17,33},{1,113},{18,34},{2,114},{19,35},{3,115},{2... | collective-permute-start | bytes 1572872 | tf_op jit(solution)/shard_map/ppermute | solution.py:240
  45.0 17.4 %collective-permute-start.12 = (f32[1024,128]{1,0:T(8,128)S(1)}, f32[1024,128]{1,0:T(8,128)S(1)}, u32[]{:S(2)}, u32[]{:S(2)}) collective-permute-start(f32[1024,128]{1,0:T(8,128)S(1)} %select_select_fusion.2), channel_id=1, source_target_pairs={{64,48},{96,112},{48,32},{80,96},{65,49},{97,113},{49,33},{81,97},... | collective-permute-start | bytes 1572872 | tf_op jit(solution)/shard_map/ppermute | solution.py:240
  46.9 15.8 %collective-permute-start.11 = (f32[1024,128]{1,0:T(8,128)S(1)}, f32[1024,128]{1,0:T(8,128)S(1)}, u32[]{:S(2)}, u32[]{:S(2)}) collective-permute-start(f32[1024,128]{1,0:T(8,128)S(1)} %get-tuple-element.32.own_rows), channel_id=1, source_target_pairs={{0,128},{128,0},{1,129},{129,1},{2,130},{130,2},{3,131},{131,3},{4... | collective-permute-start | bytes 1572872 | tf_op jit(solution)/shard_map/ppermute | solution.py:237

commit v6 on v5

--- a/solution.py
+++ b/solution.py
@@ -279,24 +279,24 @@
     mine = jnp.stack(both_of(tile, *near(tile)))
     x_a, mine = lax.optimization_barrier((x_a, mine))
     held = choose(col, [(x_a, ()), (strip, (0, 1))])
-    x_b = send(held, [(0, 1), (5, 4), (4, 3)])
-    x_c = send(held, [(1, 0), (5, 6), (4, 5)])
+    x_b = send(held, [(0, 1), (5, 6), (4, 3)])
+    x_c = send(held, [(1, 0), (5, 4), (4, 5)])
     own = jnp.stack(
         [mine] + [lax.ppermute(mine, "depth", [(d, (d + 4 * j) % 16) for d in range(16)]) for j in (1, 2, 3)]
     )
-    x_b, x_c, own = lax.optimization_barrier((x_b, x_c, own))
+    x_c, x_b, own = lax.optimization_barrier((x_c, x_b, own))
     other = swap(own)
 
     own, other, own_rows = lax.optimization_barrier((own, other, own_rows))
     other_rows = swap(own_rows)
-    held = choose(col, [(x_b, ()), (x_c, (0, 5, 6))])
+    held = choose(col, [(x_b, ()), (x_c, (0, 4, 5))])
     x_d = send(held, [(4, 3), (6, 7), (3, 2), (5, 6)])
     x_e = send(held, [(1, 2), (0, 7)])
     inv0, up, inv1 = call(
         second_kernel, ids, (own, other), [whole(own.shape)] * 2, [(NB, NB)] * 3, scratch[:1] + scratch, 10**10, 12
     )
     x_d, x_e, inv1 = lax.optimization_barrier((x_d, x_e, inv1))
-    x0 = choose(col, [(x_d, ()), (strip, (0,)), (x_b, (1, 4)), (x_e, (2,)), (x_a, (5,)), (x_c, (6,))])
+    x0 = choose(col, [(x_d, ()), (strip, (0,)), (x_b, (1, 6)), (x_e, (2,)), (x_a, (5,)), (x_c, (4,))])
     x1 = choose(col, [(x_d, ()), (x_c, (0, 5)), (strip, (1,)), (x_b, (3,)), (x_a, (4,)), (x_e, (7,))])
     (out,) = call(
         last_kernel,

time: 69.9 us -> 68.1 us (0.974)
  waiting for transfers between devices: 31.6 us -> 29.8 us
    ppermute x9, waiting for transfers between devices: 24.3 us -> 22.4 us  [send(): return lax.ppermute(x, 'col', pairs)]
where the time goes in v6:
time: 68.1 us; the launch traced here: 67.9 us
  waiting for transfers between devices  29.8 us (44%)
  Pallas kernels  20.9 us (31%)
  starting transfers between devices  16.2 us (24%)
    ppermute x9, waiting for transfers between devices, send(): return lax.ppermute(x, 'col', pairs)  22.4 us
    pallas_call x3, Pallas kernels, call(): pl.pallas_call(kernel, out_shape=[jax.ShapeDtypeStruct(s, jnp.float32) fo...  20.9 us
    ppermute x9, starting transfers between devices, send(): return lax.ppermute(x, 'col', pairs)  10.9 us
    ppermute x3, waiting for transfers between devices, shards(): lax.ppermute(mine, 'depth', [(d, (d + 4 * j) % 16) for d in range(16)])  7.32 us
    ppermute x3, starting transfers between devices, shards(): lax.ppermute(mine, 'depth', [(d, (d + 4 * j) % 16) for d in range(16)])  4.7 us
  transfers between devices with their start and end apart: 14, of which 8 were waited for; matrix products, arithmetic and copies ran while one was open for 1% of the time, Pallas kernels for 17%

profile of v6, /device:TPU:100, one launch (start us, length us, event | category | flops | bytes accessed | tf_op | source)
XLA Modules:
  0.0 67.9 jit_solution(6458357834899785443)
XLA Ops:
  0.0 0.1 pad_add_fusion.ids
  0.1 1.9 %shard_map.17 = (f32[512,128]{1,0:T(8,128)S(1)}, f32[1024,128]{1,0:T(8,128)S(1)}, f32[2048,128]{1,0:T(8,128)S(1)}) custom-call(s32[3]{0:T(128)S(1)} %pad_add_fusion.ids, f32[32768,128]{1,0:T(8,128)} %bitcast.27), custom_call_target="tpu_custom_call" | custom-call | flops 10000000000 | bytes 1048576 | tf_op jit(solution)/shard_map/pallas_call | solution.py:206
  2.1 0.2 slice.8
  2.3 1.3 %collective-permute-start.2 = (f32[128,128]{1,0:T(8,128)S(1)}, f32[128,128]{1,0:T(8,128)S(1)}, u32[]{:S(2)}, u32[]{:S(2)}) collective-permute-start(f32[128,128]{1,0:T(8,128)S(1)} %dynamic-slice_select_fusion), channel_id=1, source_target_pairs={{0,48},{16,64},{1,49},{17,65},{2,50},{18,66},{3,51},{19,67},{4,52}... | collective-permute-start | bytes 196616 | tf_op jit(solution)/shard_map/ppermute | solution.py:240
  3.6 0.7 collective-permute-start.1
  4.3 0.7 %collective-permute-start = (f32[1024,128]{1,0:T(8,128)S(1)}, f32[1024,128]{1,0:T(8,128)S(1)}, u32[]{:S(2)}, u32[]{:S(2)}) collective-permute-start(f32[1024,128]{1,0:T(8,128)S(1)} %bitcast.18), channel_id=1, source_target_pairs={{0,80},{16,64},{1,81},{17,65},{2,82},{18,66},{3,83},{19,67},{4,84}... | collective-permute-start | bytes 1572872 | tf_op jit(solution)/shard_map/ppermute | solution.py:240
  5.0 9.8 %collective-permute-done.2 = f32[128,128]{1,0:T(8,128)S(1)} collective-permute-done((f32[128,128]{1,0:T(8,128)S(1)}, f32[128,128]{1,0:T(8,128)S(1)}, u32[]{:S(2)}, u32[]{:S(2)}) %collective-permute-start.2) | collective-permute-done | bytes 65568 | tf_op jit(solution)/shard_map/ppermute | solution.py:240
  14.8 0.0 collective-permute-done.1
  14.8 1.8 %collective-permute-start.4 = (f32[128,128]{1,0:T(8,128)S(1)}, f32[128,128]{1,0:T(8,128)S(1)}, u32[]{:S(2)}, u32[]{:S(2)}) collective-permute-start(f32[128,128]{1,0:T(8,128)S(1)} %select_select_fusion.8), channel_id=1, source_target_pairs={{0,16},{48,64},{80,96},{16,32},{64,80},{96,112},{1,17},{49,65},{81... | collective-permute-start | bytes 196616 | tf_op jit(solution)/shard_map/ppermute | solution.py:240
  16.5 1.9 %collective-permute-start.3 = (f32[128,128]{1,0:T(8,128)S(1)}, f32[128,128]{1,0:T(8,128)S(1)}, u32[]{:S(2)}, u32[]{:S(2)}) collective-permute-start(f32[128,128]{1,0:T(8,128)S(1)} %select_select_fusion.8), channel_id=1, source_target_pairs={{0,112},{48,32},{16,0},{64,48},{1,113},{49,33},{17,1},{65,49},{2,1... | collective-permute-start | bytes 196616 | tf_op jit(solution)/shard_map/ppermute | solution.py:240
  18.5 6.6 %collective-permute-done.4 = f32[128,128]{1,0:T(8,128)S(1)} collective-permute-done((f32[128,128]{1,0:T(8,128)S(1)}, f32[128,128]{1,0:T(8,128)S(1)}, u32[]{:S(2)}, u32[]{:S(2)}) %collective-permute-start.4) | collective-permute-done | bytes 65568 | tf_op jit(solution)/shard_map/ppermute | solution.py:240
  25.1 0.3 collective-permute-done.3
  25.5 0.1 select_select_fusion.3
  25.5 1.3 %collective-permute-start.6 = (f32[1024,128]{1,0:T(8,128)S(1)}, f32[1024,128]{1,0:T(8,128)S(1)}, u32[]{:S(2)}, u32[]{:S(2)}) collective-permute-start(f32[1024,128]{1,0:T(8,128)S(1)} %select_select_fusion.3), channel_id=1, source_target_pairs={{0,16},{80,96},{64,48},{1,17},{81,97},{65,49},{2,18},{82,98},{66,5... | collective-permute-start | bytes 1572872 | tf_op jit(solution)/shard_map/ppermute | solution.py:240
  26.8 0.7 %collective-permute-start.5 = (f32[1024,128]{1,0:T(8,128)S(1)}, f32[1024,128]{1,0:T(8,128)S(1)}, u32[]{:S(2)}, u32[]{:S(2)}) collective-permute-start(f32[1024,128]{1,0:T(8,128)S(1)} %select_select_fusion.3), channel_id=1, source_target_pairs={{16,0},{80,64},{64,80},{17,1},{81,65},{65,81},{18,2},{82,66},{66,8... | collective-permute-start | bytes 1572872 | tf_op jit(solution)/shard_map/ppermute | solution.py:240
  27.5 3.1 %collective-permute-start.9 = (f32[2,128,128]{2,1,0:T(8,128)S(1)}, f32[2,128,128]{2,1,0:T(8,128)S(1)}, u32[]{:S(2)}, u32[]{:S(2)}) collective-permute-start(f32[2,128,128]{2,1,0:T(8,128)S(1)} %pad_maximum_fusion.1), channel_id=1, source_target_pairs={{0,12},{1,13},{2,14},{3,15},{4,0},{5,1},{6,2},{7,3},{8,4},{9,5},{1... | collective-permute-start | bytes 393224 | tf_op jit(solution)/shard_map/ppermute | solution.py:285
  30.6 0.6 collective-permute-start.8
  31.3 1.0 %collective-permute-start.7 = (f32[2,128,128]{2,1,0:T(8,128)S(1)}, f32[2,128,128]{2,1,0:T(8,128)S(1)}, u32[]{:S(2)}, u32[]{:S(2)}) collective-permute-start(f32[2,128,128]{2,1,0:T(8,128)S(1)} %pad_maximum_fusion.1), channel_id=1, source_target_pairs={{0,4},{1,5},{2,6},{3,7},{4,8},{5,9},{6,10},{7,11},{8,12},{9,13},{1... | collective-permute-start | bytes 393224 | tf_op jit(solution)/shard_map/ppermute | solution.py:285
  32.2 3.6 %collective-permute-done.9 = f32[2,128,128]{2,1,0:T(8,128)S(1)} collective-permute-done((f32[2,128,128]{2,1,0:T(8,128)S(1)}, f32[2,128,128]{2,1,0:T(8,128)S(1)}, u32[]{:S(2)}, u32[]{:S(2)}) %collective-permute-start.9) | collective-permute-done | bytes 131104 | tf_op jit(solution)/shard_map/ppermute | solution.py:285
  35.9 2.3 %collective-permute-done.8 = f32[2,128,128]{2,1,0:T(8,128)S(1)} collective-permute-done((f32[2,128,128]{2,1,0:T(8,128)S(1)}, f32[2,128,128]{2,1,0:T(8,128)S(1)}, u32[]{:S(2)}, u32[]{:S(2)}) %collective-permute-start.8) | collective-permute-done | bytes 131104 | tf_op jit(solution)/shard_map/ppermute | solution.py:285
  38.2 1.4 %collective-permute-done.7 = f32[2,128,128]{2,1,0:T(8,128)S(1)} collective-permute-done((f32[2,128,128]{2,1,0:T(8,128)S(1)}, f32[2,128,128]{2,1,0:T(8,128)S(1)}, u32[]{:S(2)}, u32[]{:S(2)}) %collective-permute-start.7) | collective-permute-done | bytes 131104 | tf_op jit(solution)/shard_map/ppermute | solution.py:285
  39.6 2.6 %collective-permute-done.6 = f32[1024,128]{1,0:T(8,128)S(1)} collective-permute-done((f32[1024,128]{1,0:T(8,128)S(1)}, f32[1024,128]{1,0:T(8,128)S(1)}, u32[]{:S(2)}, u32[]{:S(2)}) %collective-permute-start.6) | collective-permute-done | bytes 524320 | tf_op jit(solution)/shard_map/ppermute | solution.py:240
  42.2 0.0 collective-permute-done.5
  42.2 0.0 collective-permute-start.10
  42.2 0.1 select_select_fusion.2
  42.3 0.7 %collective-permute-start.13 = (f32[1024,128]{1,0:T(8,128)S(1)}, f32[1024,128]{1,0:T(8,128)S(1)}, u32[]{:S(2)}, u32[]{:S(2)}) collective-permute-start(f32[1024,128]{1,0:T(8,128)S(1)} %select_select_fusion.2), channel_id=1, source_target_pairs={{16,32},{0,112},{17,33},{1,113},{18,34},{2,114},{19,35},{3,115},{2... | collective-permute-start | bytes 1572872 | tf_op jit(solution)/shard_map/ppermute | solution.py:240
  43.0 1.9 %collective-permute-start.12 = (f32[1024,128]{1,0:T(8,128)S(1)}, f32[1024,128]{1,0:T(8,128)S(1)}, u32[]{:S(2)}, u32[]{:S(2)}) collective-permute-start(f32[1024,128]{1,0:T(8,128)S(1)} %select_select_fusion.2), channel_id=1, source_target_pairs={{64,48},{96,112},{48,32},{80,96},{65,49},{97,113},{49,33},{81,97},... | collective-permute-start | bytes 1572872 | tf_op jit(solution)/shard_map/ppermute | solution.py:240
  44.9 0.6 collective-permute-start.11
  45.5 11.9 %shard_map.18 = (f32[256,256]{1,0:T(8,128)S(1)}, f32[256,256]{1,0:T(8,128)S(1)}, f32[256,256]{1,0:T(8,128)S(1)}) custom-call(s32[3]{0:T(128)S(1)} %pad_add_fusion.ids, f32[4,2,128,128]{3,2,1,0:T(8,128)S(1)} %pad_maximum_fusion.own, f32[4,2,128,128]{3,2,1,0:T(8,128)S(1)} %collective-permute-done.10.other), custom_call_target="tpu_custom_call" | custom-call | flops 10000000000 | bytes 1048576 | tf_op jit(solution)/shard_map/pallas_call | solution.py:206
  57.4 3.1 %collective-permute-done.12 = f32[1024,128]{1,0:T(8,128)S(1)} collective-permute-done((f32[1024,128]{1,0:T(8,128)S(1)}, f32[1024,128]{1,0:T(8,128)S(1)}, u32[]{:S(2)}, u32[]{:S(2)}) %collective-permute-start.12) | collective-permute-done | bytes 524320 | tf_op jit(solution)/shard_map/ppermute | solution.py:240
  60.6 0.3 fusion.6
  60.8 7.0 %shard_map.19 = f32[2048,128]{1,0:T(8,128)} custom-call(s32[3]{0:T(128)S(1)} %pad_add_fusion.ids, f32[2048,128]{1,0:T(8,128)S(1)} %get-tuple-element.24.slab, f32[1024,128]{1,0:T(8,128)S(1)} %get-tuple-element.32.own_rows, f32[1024,128]{1,0:T(8,128)S(1)} %collective-permute-done.11.other_rows, f32[1024,128]{1,0:T(8,128)S(1)} %get-tuple-element.44.x0, ...), custom_call_target="tpu_custom_call" | custom-call | flops 1000000000 | bytes 1048576 | tf_op jit(solution)/shard_map/pallas_call | solution.py:206
  (11 shorter events, 0.2 us)
Async XLA Ops:
  2.3 12.4 %collective-permute-start.2 = (f32[128,128]{1,0:T(8,128)S(1)}, f32[128,128]{1,0:T(8,128)S(1)}, u32[]{:S(2)}, u32[]{:S(2)}) collective-permute-start(f32[128,128]{1,0:T(8,128)S(1)} %dynamic-slice_select_fusion), channel_id=1, source_target_pairs={{0,48},{16,64},{1,49},{17,65},{2,50},{18,66},{3,51},{19,67},{4,52}... | collective-permute-start | bytes 196616 | tf_op jit(solution)/shard_map/ppermute | solution.py:240
  3.6 11.1 %collective-permute-start.1 = (f32[128,128]{1,0:T(8,128)S(1)}, f32[128,128]{1,0:T(8,128)S(1)}, u32[]{:S(2)}, u32[]{:S(2)}) collective-permute-start(f32[128,128]{1,0:T(8,128)S(1)} %dynamic-slice_select_fusion), channel_id=1, source_target_pairs={{0,80},{16,96},{1,81},{17,97},{2,82},{18,98},{3,83},{19,99},{4,84}... | collective-permute-start | bytes 196616 | tf_op jit(solution)/shard_map/ppermute | solution.py:240
  4.3 21.2 %collective-permute-start = (f32[1024,128]{1,0:T(8,128)S(1)}, f32[1024,128]{1,0:T(8,128)S(1)}, u32[]{:S(2)}, u32[]{:S(2)}) collective-permute-start(f32[1024,128]{1,0:T(8,128)S(1)} %bitcast.18), channel_id=1, source_target_pairs={{0,80},{16,64},{1,81},{17,65},{2,82},{18,66},{3,83},{19,67},{4,84}... | collective-permute-start | bytes 1572872 | tf_op jit(solution)/shard_map/ppermute | solution.py:240
  14.8 10.3 %collective-permute-start.4 = (f32[128,128]{1,0:T(8,128)S(1)}, f32[128,128]{1,0:T(8,128)S(1)}, u32[]{:S(2)}, u32[]{:S(2)}) collective-permute-start(f32[128,128]{1,0:T(8,128)S(1)} %select_select_fusion.8), channel_id=1, source_target_pairs={{0,16},{48,64},{80,96},{16,32},{64,80},{96,112},{1,17},{49,65},{81... | collective-permute-start | bytes 196616 | tf_op jit(solution)/shard_map/ppermute | solution.py:240
  16.5 8.9 %collective-permute-start.3 = (f32[128,128]{1,0:T(8,128)S(1)}, f32[128,128]{1,0:T(8,128)S(1)}, u32[]{:S(2)}, u32[]{:S(2)}) collective-permute-start(f32[128,128]{1,0:T(8,128)S(1)} %select_select_fusion.8), channel_id=1, source_target_pairs={{0,112},{48,32},{16,0},{64,48},{1,113},{49,33},{17,1},{65,49},{2,1... | collective-permute-start | bytes 196616 | tf_op jit(solution)/shard_map/ppermute | solution.py:240
  25.5 16.7 %collective-permute-start.6 = (f32[1024,128]{1,0:T(8,128)S(1)}, f32[1024,128]{1,0:T(8,128)S(1)}, u32[]{:S(2)}, u32[]{:S(2)}) collective-permute-start(f32[1024,128]{1,0:T(8,128)S(1)} %select_select_fusion.3), channel_id=1, source_target_pairs={{0,16},{80,96},{64,48},{1,17},{81,97},{65,49},{2,18},{82,98},{66,5... | collective-permute-start | bytes 1572872 | tf_op jit(solution)/shard_map/ppermute | solution.py:240
  26.8 15.4 %collective-permute-start.5 = (f32[1024,128]{1,0:T(8,128)S(1)}, f32[1024,128]{1,0:T(8,128)S(1)}, u32[]{:S(2)}, u32[]{:S(2)}) collective-permute-start(f32[1024,128]{1,0:T(8,128)S(1)} %select_select_fusion.3), channel_id=1, source_target_pairs={{16,0},{80,64},{64,80},{17,1},{81,65},{65,81},{18,2},{82,66},{66,8... | collective-permute-start | bytes 1572872 | tf_op jit(solution)/shard_map/ppermute | solution.py:240
  27.5 8.3 %collective-permute-start.9 = (f32[2,128,128]{2,1,0:T(8,128)S(1)}, f32[2,128,128]{2,1,0:T(8,128)S(1)}, u32[]{:S(2)}, u32[]{:S(2)}) collective-permute-start(f32[2,128,128]{2,1,0:T(8,128)S(1)} %pad_maximum_fusion.1), channel_id=1, source_target_pairs={{0,12},{1,13},{2,14},{3,15},{4,0},{5,1},{6,2},{7,3},{8,4},{9,5},{1... | collective-permute-start | bytes 393224 | tf_op jit(solution)/shard_map/ppermute | solution.py:285
  30.6 7.6 %collective-permute-start.8 = (f32[2,128,128]{2,1,0:T(8,128)S(1)}, f32[2,128,128]{2,1,0:T(8,128)S(1)}, u32[]{:S(2)}, u32[]{:S(2)}) collective-permute-start(f32[2,128,128]{2,1,0:T(8,128)S(1)} %pad_maximum_fusion.1), channel_id=1, source_target_pairs={{0,8},{1,9},{2,10},{3,11},{4,12},{5,13},{6,14},{7,15},{8,0},{9,1},... | collective-permute-start | bytes 393224 | tf_op jit(solution)/shard_map/ppermute | solution.py:285
  31.3 8.3 %collective-permute-start.7 = (f32[2,128,128]{2,1,0:T(8,128)S(1)}, f32[2,128,128]{2,1,0:T(8,128)S(1)}, u32[]{:S(2)}, u32[]{:S(2)}) collective-permute-start(f32[2,128,128]{2,1,0:T(8,128)S(1)} %pad_maximum_fusion.1), channel_id=1, source_target_pairs={{0,4},{1,5},{2,6},{3,7},{4,8},{5,9},{6,10},{7,11},{8,12},{9,13},{1... | collective-permute-start | bytes 393224 | tf_op jit(solution)/shard_map/ppermute | solution.py:285
  42.2 2.7 %collective-permute-start.10 = (f32[4,2,128,128]{3,2,1,0:T(8,128)S(1)}, f32[4,2,128,128]{3,2,1,0:T(8,128)S(1)}, u32[]{:S(2)}, u32[]{:S(2)}) collective-permute-start(f32[4,2,128,128]{3,2,1,0:T(8,128)S(1)} %pad_maximum_fusion.own), channel_id=1, source_target_pairs={{0,128},{128,0},{1,129},{129,1},{2,130},{130,2},{3,131},{131,3},{4... | collective-permute-start | bytes 1572872 | tf_op jit(solution)/shard_map/ppermute | solution.py:237
  42.3 15.1 %collective-permute-start.13 = (f32[1024,128]{1,0:T(8,128)S(1)}, f32[1024,128]{1,0:T(8,128)S(1)}, u32[]{:S(2)}, u32[]{:S(2)}) collective-permute-start(f32[1024,128]{1,0:T(8,128)S(1)} %select_select_fusion.2), channel_id=1, source_target_pairs={{16,32},{0,112},{17,33},{1,113},{18,34},{2,114},{19,35},{3,115},{2... | collective-permute-start | bytes 1572872 | tf_op jit(solution)/shard_map/ppermute | solution.py:240
  43.0 17.6 %collective-permute-start.12 = (f32[1024,128]{1,0:T(8,128)S(1)}, f32[1024,128]{1,0:T(8,128)S(1)}, u32[]{:S(2)}, u32[]{:S(2)}) collective-permute-start(f32[1024,128]{1,0:T(8,128)S(1)} %select_select_fusion.2), channel_id=1, source_target_pairs={{64,48},{96,112},{48,32},{80,96},{65,49},{97,113},{49,33},{81,97},... | collective-permute-start | bytes 1572872 | tf_op jit(solution)/shard_map/ppermute | solution.py:240
  44.9 15.9 %collective-permute-start.11 = (f32[1024,128]{1,0:T(8,128)S(1)}, f32[1024,128]{1,0:T(8,128)S(1)}, u32[]{:S(2)}, u32[]{:S(2)}) collective-permute-start(f32[1024,128]{1,0:T(8,128)S(1)} %get-tuple-element.32.own_rows), channel_id=1, source_target_pairs={{0,128},{128,0},{1,129},{129,1},{2,130},{130,2},{3,131},{131,3},{4... | collective-permute-start | bytes 1572872 | tf_op jit(solution)/shard_map/ppermute | solution.py:237
